TPU v7x, 128 devices: a whole 4x4x4 slice. The times are simulated.
128 devices in a mesh: gx: 8 (over y, core), gy: 16 (over z, x).
Axes of the slice: x: 4, y: 4, z: 4, core: 2. Of those that a mesh axis runs over, the one named last changes fastest.
Arguments:
- pressure: float32 [256, 512, 128], P('gx', 'gy'), may hold values from 0.5 to 1.5
- water_sat: float32 [256, 512, 128], P('gx', 'gy'), may hold values from 0.1 to 0.5
- gas_sat: float32 [256, 512, 128], P('gx', 'gy'), may hold values from 0.05 to 0.4
- old_content: float32 [3, 256, 512, 128], P(None, 'gx', 'gy'), may hold values from 0.05 to 0.6
- pore_volume: float32 [256, 512, 128], P('gx', 'gy'), may hold values from 0.2 to 2
- trans_x: float32 [256, 512, 128], P('gx', 'gy'), may hold values from 0.05 to 2
- trans_y: float32 [256, 512, 128], P('gx', 'gy'), may hold values from 0.05 to 2
- trans_z: float32 [256, 512, 128], P('gx', 'gy'), may hold values from 0.05 to 2
- active: int32 [256, 512, 128], P('gx', 'gy'), may hold values 0 or 1
- aggregate: int32 [256, 512, 128], P('gx', 'gy'), may hold values from 0 to 7, as said below
- well_cells: int32 [512, 16], P(('gx', 'gy')), may hold values from -1 to 16777215, as said below
- well_index: float32 [512, 16], P(('gx', 'gy')), may hold values from 0.5 to 5
- bottom_hole: float32 [512], P(('gx', 'gy')), may hold values from 0.3 to 1.8
- well_target: float32 [512], P(('gx', 'gy')), may hold values from -24 to 24
Outputs:
- residual: float32 [3, 256, 512, 128], P(None, 'gx', 'gy')
- pressure_update: float32 [256, 512, 128], P('gx', 'gy')
- well_residual: float32 [512], P(('gx', 'gy'))
Inputs may be any that keep to these rules, and one draw needn't show every extreme that they name: `well_cells`: each row lists distinct cells of one well on consecutive layers, one a layer, then -1 in the remaining slots; every well has at least one cell and some well fills all 16 slots. `aggregate`: within every vertical column the value never falls with depth and every value appears.
All inputs are finite; a program needn't handle non-finite values. No bound on the sum of `active` on one device may be relied on, other than what follows from the above.
Results may differ from a plain program's by a relative error of at most 0.0003.
Values sent between devices are 32-bit elements; how exact they have to be, the bound alone decides.
A program may use at most 128 MiB of HBM per device.

v0:
```python
import jax
import jax.numpy as jnp
from jax import lax
from jax.sharding import PartitionSpec as P

AGG_DEV = 8
CITERS = 24


precise = lax.Precision.HIGHEST
compress = (0.001, 0.001, 0.005)
viscosity = (0.5, 1.5, 0.2)
density = (1.0, 0.8, 0.2)
gravity_step = 0.05
relax = 0.6
dead_leak = 0.001


def extended(value, sides, width):
    for axis, dim in sides:
        count, length = (lax.axis_size(axis), value.shape[dim])
        up = [(i, (i + 1) % count) for i in range(count - 1)]
        down = [(j, i) for i, j in up]
        last = lax.slice_in_dim(value, length - width, length, axis=dim)
        first = lax.slice_in_dim(value, 0, width, axis=dim)
        before = lax.ppermute(last, axis, up)
        after = lax.ppermute(first, axis, down)
        value = jnp.concatenate([before, value, after], axis=dim)
    return value


def phase_mobility(pressure, water_sat, gas_sat):
    oil_sat = 1.0 - water_sat - gas_sat
    saturation = (water_sat, oil_sat, gas_sat)
    factors = tuple((1.0 + compress[k] * (pressure - 1.0) for k in range(3)))
    mobility = tuple((factors[k] * saturation[k] * saturation[k] / viscosity[k] for k in range(3)))
    return (saturation, factors, mobility)


def mean_flux(face_trans, mob_low, mob_high, potential):
    return face_trans * (0.5 * (mob_low + mob_high)) * potential


def shifted(padded, rows_x, rows_y, step_x, step_y):
    return padded[:, 1 + step_x : 1 + step_x + rows_x, 1 + step_y : 1 + step_y + rows_y]


def along_depth(values):
    return (jnp.pad(values, ((0, 0), (0, 0), (0, 1))), jnp.pad(values, ((0, 0), (0, 0), (1, 0))))


def coupling(member, weight, partner_ids, groups):
    labels = jnp.arange(groups, dtype=jnp.int32)[:, None, None, None]
    partner = (partner_ids[None] == labels).astype(jnp.float32).reshape(groups, -1)
    return jnp.einsum("ac,bc->ab", member * weight.reshape(1, -1), partner, precision=precise)


def coarse_solve(matrix, rhs_all):

    def one_step(step, carry):
        solution, rest, search, norm_now = carry
        image = jnp.dot(matrix, search, precision=precise)
        alpha = norm_now / jnp.sum(search * image)
        solution = solution + alpha * search
        rest = rest - alpha * image
        norm_next = jnp.sum(rest * rest)
        search = rest + norm_next / norm_now * search
        return (solution, rest, search, norm_next)

    start = (jnp.zeros_like(rhs_all), rhs_all, rhs_all, jnp.sum(rhs_all * rhs_all))
    return lax.fori_loop(0, CITERS, one_step, start)[0]


def per_device(
    pressure,
    water_sat,
    gas_sat,
    old_content,
    pore_volume,
    trans_x,
    trans_y,
    trans_z,
    active,
    aggregate,
    well_cells,
    well_index,
    bottom_hole,
    well_target,
):
    rows_x, rows_y, layers = pressure.shape
    across_x = lax.axis_size("gx")
    across_y = lax.axis_size("gy")
    place_x = lax.axis_index("gx")
    place_y = lax.axis_index("gy")
    device = place_x * across_y + place_y
    groups = AGG_DEV
    devices_all = across_x * across_y
    total_aggs = groups * devices_all
    cell_count = rows_x * rows_y * layers
    live_mask = active.astype(jnp.float32)
    stacked = jnp.stack(
        [pressure, water_sat, gas_sat, live_mask, trans_x, trans_y, aggregate.astype(jnp.float32)]
    )
    padded = extended(stacked, (("gx", 1), ("gy", 2)), 1)
    upper_x = shifted(padded, rows_x, rows_y, 1, 0)
    lower_x = shifted(padded, rows_x, rows_y, -1, 0)
    upper_y = shifted(padded, rows_x, rows_y, 0, 1)
    lower_y = shifted(padded, rows_x, rows_y, 0, -1)
    saturation, factors, mobility = phase_mobility(pressure, water_sat, gas_sat)
    mob_upper_x = phase_mobility(upper_x[0], upper_x[1], upper_x[2])[2]
    mob_lower_x = phase_mobility(lower_x[0], lower_x[1], lower_x[2])[2]
    mob_upper_y = phase_mobility(upper_y[0], upper_y[1], upper_y[2])[2]
    mob_lower_y = phase_mobility(lower_y[0], lower_y[1], lower_y[2])[2]
    face_upper_x = trans_x * live_mask * upper_x[3]
    face_lower_x = lower_x[4] * lower_x[3] * live_mask
    face_upper_y = trans_y * live_mask * upper_y[3]
    face_lower_y = lower_y[5] * lower_y[3] * live_mask
    face_z = trans_z[:, :, :-1] * live_mask[:, :, :-1] * live_mask[:, :, 1:]
    total_mob = mobility[0] + mobility[1] + mobility[2]
    cells_all = lax.all_gather(well_cells, ("gx", "gy"), axis=0, tiled=True)
    index_all, hole_all = (
        lax.all_gather(well_index, ("gx", "gy"), axis=0, tiled=True),
        lax.all_gather(bottom_hole, ("gx", "gy"), axis=0, tiled=True),
    )
    flat_cells = cells_all.reshape(-1)
    span_y = rows_y * across_y
    plane_size = span_y * layers
    cell_x = flat_cells // plane_size
    cell_y = flat_cells // layers % span_y
    cell_z = flat_cells % layers
    owned_here = (flat_cells >= 0) & (cell_x // rows_x == place_x) & (cell_y // rows_y == place_y)
    local_index = jnp.where(
        owned_here, cell_x % rows_x * (rows_y * layers) + cell_y % rows_y * layers + cell_z, 0
    )
    perf_press = pressure.reshape(-1)[local_index]
    strength = jnp.where(
        owned_here, index_all.reshape(-1) * live_mask.reshape(-1)[local_index], 0.0
    )
    hole_press = jnp.broadcast_to(hole_all[:, None], cells_all.shape).reshape(-1)
    drawdown = hole_press - perf_press
    phase_rates = [strength * mobility[k].reshape(-1)[local_index] * drawdown for k in range(3)]
    perf_total = phase_rates[0] + phase_rates[1] + phase_rates[2]
    well_partial = jnp.sum(perf_total.reshape(cells_all.shape), axis=1)
    well_residual = (
        lax.psum_scatter(well_partial, ("gx", "gy"), scatter_dimension=0, tiled=True) - well_target
    )
    residuals = []
    for k in range(3):
        net_x = mean_flux(
            face_upper_x, mobility[k], mob_upper_x[k], pressure - upper_x[0]
        ) - mean_flux(face_lower_x, mob_lower_x[k], mobility[k], lower_x[0] - pressure)
        net_y = mean_flux(
            face_upper_y, mobility[k], mob_upper_y[k], pressure - upper_y[0]
        ) - mean_flux(face_lower_y, mob_lower_y[k], mobility[k], lower_y[0] - pressure)
        high_z, low_z = along_depth(
            mean_flux(
                face_z,
                mobility[k][:, :, :-1],
                mobility[k][:, :, 1:],
                pressure[:, :, :-1] - pressure[:, :, 1:] + density[k] * gravity_step,
            )
        )
        net_z = high_z - low_z
        source = (
            jnp.zeros((cell_count,), jnp.float32)
            .at[local_index]
            .add(phase_rates[k])
            .reshape(pressure.shape)
        )
        stored = pore_volume * (factors[k] * saturation[k] - old_content[k])
        residuals.append(live_mask * (stored + (net_x + net_y + net_z)) - source)
    total_upper_x = mob_upper_x[0] + mob_upper_x[1] + mob_upper_x[2]
    total_lower_x = mob_lower_x[0] + mob_lower_x[1] + mob_lower_x[2]
    total_upper_y = mob_upper_y[0] + mob_upper_y[1] + mob_upper_y[2]
    total_lower_y = mob_lower_y[0] + mob_lower_y[1] + mob_lower_y[2]
    coef_upper_x = face_upper_x * (0.5 * (total_mob + total_upper_x))
    coef_lower_x = face_lower_x * (0.5 * (total_lower_x + total_mob))
    coef_upper_y = face_upper_y * (0.5 * (total_mob + total_upper_y))
    coef_lower_y = face_lower_y * (0.5 * (total_lower_y + total_mob))
    coef_z = face_z * (0.5 * (total_mob[:, :, :-1] + total_mob[:, :, 1:]))
    coef_upper_z, coef_lower_z = along_depth(coef_z)
    well_diag = (
        jnp.zeros((cell_count,), jnp.float32)
        .at[local_index]
        .add(strength * total_mob.reshape(-1)[local_index])
        .reshape(pressure.shape)
    )
    storage = pore_volume * (
        compress[0] * saturation[0] + compress[1] * saturation[1] + compress[2] * saturation[2]
    )
    leak = live_mask * (storage + well_diag) + dead_leak * (1.0 - live_mask)
    diagonal = (
        coef_upper_x
        + coef_lower_x
        + (coef_upper_y + coef_lower_y)
        + (coef_upper_z + coef_lower_z)
        + leak
    )

    def apply_operator(values):
        framed = extended(values, (("gx", 0), ("gy", 1)), 1)
        above_z, below_z = (along_depth(values[:, :, 1:])[0], along_depth(values[:, :, :-1])[1])
        neighbour_sum = (
            coef_upper_x * framed[2:, 1:-1]
            + coef_lower_x * framed[:-2, 1:-1]
            + (coef_upper_y * framed[1:-1, 2:] + coef_lower_y * framed[1:-1, :-2])
            + (coef_upper_z * above_z + coef_lower_z * below_z)
        )
        return diagonal * values - neighbour_sum

    labels = jnp.arange(groups, dtype=jnp.int32)[:, None, None, None]
    member_full = (aggregate[None] == labels).astype(jnp.float32)
    member = member_full.reshape(groups, -1)
    agg_upper_x = upper_x[6].astype(jnp.int32)
    agg_lower_x = lower_x[6].astype(jnp.int32)
    agg_upper_y = upper_y[6].astype(jnp.int32)
    agg_lower_y = lower_y[6].astype(jnp.int32)
    agg_upper_z = along_depth(aggregate[:, :, 1:])[0]
    agg_lower_z = along_depth(aggregate[:, :, :-1])[1]
    index_x = jnp.arange(rows_x)[:, None, None]
    index_y = jnp.arange(rows_y)[None, :, None]
    edge_upper_x = index_x == rows_x - 1
    edge_lower_x = index_x == 0
    edge_upper_y = index_y == rows_y - 1
    edge_lower_y = index_y == 0

    def inside(coef, partner_ids, edge):
        return jnp.where(edge, 0.0, jnp.where(aggregate != partner_ids, coef, 0.0))

    self_block = coupling(
        member, inside(coef_upper_x, agg_upper_x, edge_upper_x), agg_upper_x, groups
    )
    self_block = self_block + coupling(
        member, inside(coef_lower_x, agg_lower_x, edge_lower_x), agg_lower_x, groups
    )
    self_block = self_block + coupling(
        member, inside(coef_upper_y, agg_upper_y, edge_upper_y), agg_upper_y, groups
    )
    self_block = self_block + coupling(
        member, inside(coef_lower_y, agg_lower_y, edge_lower_y), agg_lower_y, groups
    )
    self_block = self_block + coupling(
        member, jnp.where(aggregate != agg_upper_z, coef_upper_z, 0.0), agg_upper_z, groups
    )
    self_block = self_block + coupling(
        member, jnp.where(aggregate != agg_lower_z, coef_lower_z, 0.0), agg_lower_z, groups
    )
    slot_upper_x = coupling(member, jnp.where(edge_upper_x, coef_upper_x, 0.0), agg_upper_x, groups)
    slot_lower_x = coupling(member, jnp.where(edge_lower_x, coef_lower_x, 0.0), agg_lower_x, groups)
    slot_upper_y = coupling(member, jnp.where(edge_upper_y, coef_upper_y, 0.0), agg_upper_y, groups)
    slot_lower_y = coupling(member, jnp.where(edge_lower_y, coef_lower_y, 0.0), agg_lower_y, groups)
    cross_sum = (
        jnp.sum(self_block, 1)
        + jnp.sum(slot_upper_x, 1)
        + jnp.sum(slot_lower_x, 1)
        + jnp.sum(slot_upper_y, 1)
        + jnp.sum(slot_lower_y, 1)
    )
    leak_sum = jnp.dot(member, leak.reshape(-1), precision=precise)
    own_block = jnp.diag(leak_sum + cross_sum) - self_block
    neighbours = (device, device - across_y, device + across_y, device - 1, device + 1)
    pieces = (own_block, -slot_lower_x, -slot_upper_x, -slot_lower_y, -slot_upper_y)
    payload = jnp.zeros((groups, total_aggs), jnp.float32)
    for target, piece in zip(neighbours, pieces):
        start_col = jnp.clip(target, 0, devices_all - 1) * groups
        current = lax.dynamic_slice_in_dim(payload, start_col, groups, 1)
        payload = lax.dynamic_update_slice_in_dim(payload, current + piece, start_col, 1)
    pressure_rhs = -(residuals[0] + residuals[1] + residuals[2])
    smoothed = relax * pressure_rhs / diagonal
    remainder = pressure_rhs - apply_operator(smoothed)
    coarse_rhs = jnp.dot(member, remainder.reshape(-1), precision=precise)
    gathered, rhs_all = (
        lax.all_gather(payload, ("gx", "gy"), axis=0, tiled=True),
        lax.all_gather(coarse_rhs, ("gx", "gy"), axis=0, tiled=True),
    )
    coarse = coarse_solve(gathered, rhs_all)
    own_values = lax.dynamic_slice_in_dim(coarse, device * groups, groups)
    correction = jnp.sum(member_full * own_values[:, None, None, None], axis=0)
    corrected = smoothed + correction
    pressure_update = corrected + relax * (pressure_rhs - apply_operator(corrected)) / diagonal
    return (jnp.stack(residuals), pressure_update, well_residual)


def solution(mesh):
    in_specs = (
        P("gx", "gy", None),
        P("gx", "gy", None),
        P("gx", "gy", None),
        P(None, "gx", "gy", None),
        P("gx", "gy", None),
        P("gx", "gy", None),
        P("gx", "gy", None),
        P("gx", "gy", None),
        P("gx", "gy", None),
        P("gx", "gy", None),
        P(("gx", "gy"), None),
        P(("gx", "gy"), None),
        P(("gx", "gy")),
        P(("gx", "gy")),
    )
    out_specs = (P(None, "gx", "gy", None), P("gx", "gy", None), P(("gx", "gy")))
    return jax.shard_map(
        per_device, mesh=mesh, in_specs=in_specs, out_specs=out_specs, check_vma=False
    )
```

profile of v0, /device:TPU:1, one launch (start us, length us, event | category | flops | bytes accessed | tf_op | source)
XLA Modules:
  0.0 1355.2 jit_solution(11370343870019022430)
XLA Ops:
  18.8 60.6 %all-gather = s32[128,4,16]{2,1,0:T(4,128)S(1)} all-gather(s32[1,4,16]{2,1,0:T(4,128)S(1)} %bitcast.249), channel_id=1, replica_groups=mesh['gx'=8,'gy'=16] {'gx','gy'}, dimensions={0}, use_global_device_ids=true | all-gather | bytes 33024 | tf_op jit(solution)/shard_map/all_gather | solution.py:120
  87.0 59.3 %all-gather.1 = f32[128,4,16]{2,1,0:T(4,128)S(1)} all-gather(f32[1,4,16]{2,1,0:T(4,128)S(1)} %bitcast.250), channel_id=1, replica_groups=mesh['gx'=8,'gy'=16] {'gx','gy'}, dimensions={0}, use_global_device_ids=true | all-gather | bytes 33024 | tf_op jit(solution)/shard_map/all_gather | solution.py:122
  147.1 80.4 %gather_fusion = f32[8192]{0:T(1024)} fusion(f32[131072]{0:T(1024)S(1)} %bitcast.197, s32[8192]{0:T(1024)S(1)} %broadcast_clamp_fusion), kind=kCustom, calls=%fused_computation | custom fusion | bytes 98304 | tf_op jit(solution)/shard_map/gather | solution.py:137
  227.5 80.4 %gather_fusion.2 = f32[8192]{0:T(1024)} fusion(f32[131072]{0:T(1024)S(1)} %bitcast.195, s32[8192]{0:T(1024)S(1)} %broadcast_clamp_fusion), kind=kCustom, calls=%fused_computation.2 | custom fusion | bytes 98304 | tf_op jit(solution)/shard_map/gather | solution.py:135
  308.1 64.8 %all-reduce.14 = f32[512]{0:T(512)S(1)} all-reduce(f32[512]{0:T(512)S(1)} %dynamic-update-slice), channel_id=1, replica_groups=mesh['gx'=8,'gy'=16] {'gx','gy'}, use_global_device_ids=true, to_apply=%add.14 | all-reduce | flops 512 | bytes 4096
  387.1 80.5 %gather_fusion.5 = f32[8192]{0:T(1024)} fusion(f32[131072]{0:T(1024)S(1)} %bitcast.194, s32[8192]{0:T(1024)S(1)} %broadcast_clamp_fusion), kind=kCustom, calls=%fused_computation.5 | custom fusion | bytes 98304 | tf_op jit(solution)/shard_map/gather | solution.py:185
  467.5 80.5 %gather_fusion.3 = f32[8192]{0:T(1024)} fusion(f32[131072]{0:T(1024)S(1)} %bitcast.196, s32[8192]{0:T(1024)S(1)} %broadcast_clamp_fusion), kind=kCustom, calls=%fused_computation.3 | custom fusion | bytes 98304 | tf_op jit(solution)/shard_map/gather | solution.py:141
  548.0 80.5 %gather_fusion.1 = f32[8192]{0:T(1024)} fusion(f32[131072]{0:T(1024)S(1)} %bitcast.199, s32[8192]{0:T(1024)S(1)} %broadcast_clamp_fusion), kind=kCustom, calls=%fused_computation.1 | custom fusion | bytes 98304 | tf_op jit(solution)/shard_map/gather | solution.py:141
  628.5 80.4 %gather_fusion.4 = f32[8192]{0:T(1024)} fusion(f32[131072]{0:T(1024)S(1)} %bitcast.198, s32[8192]{0:T(1024)S(1)} %broadcast_clamp_fusion), kind=kCustom, calls=%fused_computation.4 | custom fusion | bytes 98304 | tf_op jit(solution)/shard_map/gather | solution.py:141
  724.9 57.8 %scatter_custom_fusion.1 = f32[131072]{0:T(1024)} fusion(s32[8192]{0:T(1024)} %bitcast.245, f32[8192]{0:T(1024)S(1)} %get-tuple-element.155, f32[]{:T(128)} %constant.156.clone.1), kind=kCustom, calls=%fused_computation.305 | custom fusion | flops 8192 | bytes 524800 | tf_op jit(solution)/shard_map/scatter-add | solution.py:167
  782.6 57.8 %scatter_custom_fusion.2 = f32[131072]{0:T(1024)} fusion(s32[8192]{0:T(1024)} %bitcast.246, f32[8192]{0:T(1024)S(1)} %get-tuple-element.154, f32[]{:T(128)} %constant.156.clone.1), kind=kCustom, calls=%fused_computation.303 | custom fusion | flops 8192 | bytes 524800 | tf_op jit(solution)/shard_map/scatter-add | solution.py:167
  840.4 57.8 %scatter_custom_fusion = f32[131072]{0:T(1024)} fusion(s32[8192]{0:T(1024)} %bitcast.247, f32[8192]{0:T(1024)S(1)} %get-tuple-element.156, f32[]{:T(128)} %constant.156.clone.1), kind=kCustom, calls=%fused_computation.307 | custom fusion | flops 8192 | bytes 524800 | tf_op jit(solution)/shard_map/scatter-add | solution.py:167
  898.2 57.9 %scatter_custom_fusion.3 = f32[131072]{0:T(1024)} fusion(s32[8192]{0:T(1024)} %bitcast.248, f32[8192]{0:T(1024)S(1)} %get-tuple-element.115, f32[]{:T(128)} %constant.156.clone.1), kind=kCustom, calls=%fused_computation.301 | custom fusion | flops 8192 | bytes 524800 | tf_op jit(solution)/shard_map/scatter-add | solution.py:185
  982.5 5.8 fusion.226
  1048.2 69.8 %all-reduce.17 = (f32[1024]{0:T(1024)S(1)}, f32[512]{0:T(512)S(1)}) all-reduce(f32[1024]{0:T(1024)S(1)} %dynamic-update-slice.1, f32[512]{0:T(512)S(1)} %fusion.168), channel_id=1, replica_groups=mesh['gx'=8,'gy'=16] {'gx','gy'}, use_global_device_ids=true, to_apply=%add.15 | all-reduce | flops 1536 | bytes 12288
  1118.6 214.6 %while.17 = (s32[]{:T(128)}, f32[1024]{0:T(1024)S(1)}, f32[1024]{0:T(1024)S(1)}, f32[1024]{0:T(1024)S(1)}, f32[]{:T(128)}, /*index=5*/f32[1024,1024]{1,0:T(8,128)}, s32[]{:T(128)}, s32[]{:T(128)}) while((s32[]{:T(128)}, f32[1024]{0:T(1024)S(1)}, f32[1024]{0:T(1024)S(1)}, f32[1024]{0:T(1024)S(1)}, f32[]{:T(128)}, ...), condition=%wide.region_13.14_spmd.clone, body=%wide.region_10.13_spmd.clone.sunk | while | flops 12594179 | bytes 4243603 | solution.py:71
  1118.6 5.8 fusion.254
  1127.6 5.8 fusion.254
  1136.5 5.8 fusion.254
  1145.5 5.8 fusion.254
  1154.4 5.8 fusion.254
  1163.4 5.8 fusion.254
  1172.3 5.8 fusion.254
  1181.2 5.8 fusion.254
  1190.2 5.8 fusion.254
  1199.1 5.8 fusion.254
  1217.0 5.8 fusion.254
  1226.0 5.8 fusion.254
  1234.9 5.8 fusion.254
  1243.8 5.8 fusion.254
  1252.8 5.8 fusion.254
  1261.7 5.8 fusion.254
  (388 shorter events, 227.8 us)
Async XLA Ops:
  7.2 1111.4 %all-gather.4.cloned.1.call-start = ((), (), s32[]{:S(2)}) async-start(), calls=%async_computation | async-start | bytes 4227072 | tf_op jit(solution)/shard_map/all_gather | solution.py:273
  11.9 362.4 %collective-permute-start = (f32[7,1,32,128]{3,2,1,0:T(8,128)S(1)}, f32[7,1,32,128]{3,2,1,0:T(8,128)S(1)}, u32[]{:S(2)}, u32[]{:S(2)}) collective-permute-start(f32[7,1,32,128]{3,2,1,0:T(8,128)S(1)} %get-tuple-element.132), channel_id=1, source_target_pairs={{16,0},{32,16},{48,32},{64,48},{80,64},{96,80},{112,96},{17,1},{33... | collective-permute-start | bytes 344072 | tf_op jit(solution)/shard_map/ppermute | solution.py:27
  15.3 359.0 %collective-permute-start.1 = (f32[7,1,32,128]{3,2,1,0:T(8,128)S(1)}, f32[7,1,32,128]{3,2,1,0:T(8,128)S(1)}, u32[]{:S(2)}, u32[]{:S(2)}) collective-permute-start(f32[7,1,32,128]{3,2,1,0:T(8,128)S(1)} %get-tuple-element.131), channel_id=1, source_target_pairs={{0,16},{16,32},{32,48},{48,64},{64,80},{80,96},{96,112},{1,17},{17... | collective-permute-start | bytes 344072 | tf_op jit(solution)/shard_map/ppermute | solution.py:26
  18.7 128.3 %copy-start.25 = (s32[32,32,127]{2,1,0:T(8,128)}, s32[32,32,127]{2,1,0:T(8,128)S(1)}, u32[]{:S(2)}) copy-start(s32[32,32,127]{2,1,0:T(8,128)S(1)} %get-tuple-element.148) | copy-start | bytes 1560580
  18.8 128.3 %copy-start.27 = (s32[32,32,127]{2,1,0:T(8,128)}, s32[32,32,127]{2,1,0:T(8,128)S(1)}, u32[]{:S(2)}) copy-start(s32[32,32,127]{2,1,0:T(8,128)S(1)} %get-tuple-element.149) | copy-start | bytes 1560580
  18.8 68.2 %copy-start.91 = (f32[4,16]{1,0:T(4,128)S(1)}, f32[4,16]{1,0:T(4,128)}, u32[]{:S(2)}) copy-start(f32[4,16]{1,0:T(4,128)} %param.27) | copy-start | bytes 772
  146.2 81.3 %copy-start.37 = (f32[128,4,16]{2,1,0:T(4,128)}, f32[128,4,16]{2,1,0:T(4,128)S(1)}, u32[]{:S(2)}) copy-start(f32[128,4,16]{2,1,0:T(4,128)S(1)} %all-gather.1) | copy-start | bytes 98308
  147.1 80.4 %copy-start = (f32[32,32,128]{2,1,0:T(8,128)S(1)}, f32[32,32,128]{2,1,0:T(8,128)}, u32[]{:S(2)}) copy-start(f32[32,32,128]{2,1,0:T(8,128)} %param.16) | copy-start | bytes 1572868
  227.5 80.4 %copy-start.93 = (f32[4]{0:T(128)S(1)}, f32[4]{0:T(128)}, u32[]{:S(2)}) copy-start(f32[4]{0:T(128)} %param.28) | copy-start | bytes 52
  377.0 579.2 %collective-permute-start.3 = (f32[7,34,1,128]{3,2,1,0:T(1,128)}, f32[7,34,1,128]{3,2,1,0:T(1,128)}, u32[]{:S(2)}, u32[]{:S(2)}) collective-permute-start(f32[7,34,1,128]{3,2,1,0:T(1,128)} %get-tuple-element.129), channel_id=1, source_target_pairs={{0,1},{1,2},{2,3},{3,4},{4,5},{5,6},{6,7},{7,8},{8,9},{9,10},{10,1... | collective-permute-start | bytes 365576 | tf_op jit(solution)/shard_map/ppermute | solution.py:26
  378.9 579.8 %collective-permute-start.2 = (f32[7,34,1,128]{3,2,1,0:T(1,128)}, f32[7,34,1,128]{3,2,1,0:T(1,128)}, u32[]{:S(2)}, u32[]{:S(2)}) collective-permute-start(f32[7,34,1,128]{3,2,1,0:T(1,128)} %get-tuple-element.130), channel_id=1, source_target_pairs={{1,0},{2,1},{3,2},{4,3},{5,4},{6,5},{7,6},{8,7},{9,8},{10,9},{11,1... | collective-permute-start | bytes 365576 | tf_op jit(solution)/shard_map/ppermute | solution.py:27
  628.5 80.4 %copy-start.49 = (f32[32,32,127]{2,1,0:T(8,128)S(1)}, f32[32,32,127]{2,1,0:T(8,128)}, u32[]{:S(2)}) copy-start(f32[32,32,127]{2,1,0:T(8,128)} %get-tuple-element.114) | copy-start | bytes 1560580
  724.1 236.6 %copy-start.15 = (f32[32,32,128]{2,1,0:T(8,128)}, f32[32,32,128]{2,1,0:T(8,128)S(1)}, u32[]{:S(2)}) copy-start(f32[32,32,128]{2,1,0:T(8,128)S(1)} %get-tuple-element.82) | copy-start | bytes 1572868
  958.7 49.1 %copy-start.18 = (f32[32,32,128]{2,1,0:T(8,128)}, f32[32,32,128]{2,1,0:T(8,128)S(1)}, u32[]{:S(2)}) copy-start(f32[32,32,128]{2,1,0:T(8,128)S(1)} %get-tuple-element.94) | copy-start | bytes 1572868
  960.7 47.1 %copy-start.20 = (f32[32,32,128]{2,1,0:T(8,128)}, f32[32,32,128]{2,1,0:T(8,128)S(1)}, u32[]{:S(2)}) copy-start(f32[32,32,128]{2,1,0:T(8,128)S(1)} %get-tuple-element.88) | copy-start | bytes 1572868
  1018.8 22.9 %copy-start.14 = (f32[32,32,128]{2,1,0:T(8,128)S(1)}, f32[32,32,128]{2,1,0:T(8,128)}, u32[]{:S(2)}) copy-start(f32[32,32,128]{2,1,0:T(8,128)} %get-tuple-element.74) | copy-start | bytes 1572868
  1018.8 22.9 %copy-start.17 = (f32[32,32,128]{2,1,0:T(8,128)S(1)}, f32[32,32,128]{2,1,0:T(8,128)}, u32[]{:S(2)}) copy-start(f32[32,32,128]{2,1,0:T(8,128)} %copy-done.15) | copy-start | bytes 1572868
  1018.8 22.9 %copy-start.19 = (f32[32,32,128]{2,1,0:T(8,128)S(1)}, f32[32,32,128]{2,1,0:T(8,128)}, u32[]{:S(2)}) copy-start(f32[32,32,128]{2,1,0:T(8,128)} %copy-done.18) | copy-start | bytes 1572868
  1024.9 15.5 %copy-start.58 = (f32[32,32,128]{2,1,0:T(8,128)S(1)}, f32[32,32,128]{2,1,0:T(8,128)}, u32[]{:S(2)}) copy-start(f32[32,32,128]{2,1,0:T(8,128)} %get-tuple-element.111) | copy-start | bytes 1572868
  1024.9 15.6 %copy-start.59 = (f32[32,32,128]{2,1,0:T(8,128)S(1)}, f32[32,32,128]{2,1,0:T(8,128)}, u32[]{:S(2)}) copy-start(f32[32,32,128]{2,1,0:T(8,128)} %get-tuple-element.112) | copy-start | bytes 1572868
  1024.9 16.9 %copy-start.21 = (f32[32,32,128]{2,1,0:T(8,128)S(1)}, f32[32,32,128]{2,1,0:T(8,128)}, u32[]{:S(2)}) copy-start(f32[32,32,128]{2,1,0:T(8,128)} %copy-done.20) | copy-start | bytes 1572868
  1024.9 16.9 %copy-start.29 = (f32[32,32,128]{2,1,0:T(8,128)S(1)}, f32[32,32,128]{2,1,0:T(8,128)}, u32[]{:S(2)}) copy-start(f32[32,32,128]{2,1,0:T(8,128)} %get-tuple-element.108) | copy-start | bytes 1572868
  1024.9 16.9 %copy-start.32 = (f32[32,32,128]{2,1,0:T(8,128)S(1)}, f32[32,32,128]{2,1,0:T(8,128)}, u32[]{:S(2)}) copy-start(f32[32,32,128]{2,1,0:T(8,128)} %copy-done.31) | copy-start | bytes 1572868
  1027.1 6.3 collective-permute-start.4
  1030.2 3.8 collective-permute-start.5
  1034.0 7.7 collective-permute-start.6
  1035.3 6.4 collective-permute-start.7
  1118.6 220.9 %copy-start.92 = (f32[4]{0:T(128)S(1)}, f32[4]{0:T(128)}, u32[]{:S(2)}) copy-start(f32[4]{0:T(128)} %param.29) | copy-start | bytes 52
  1334.0 6.2 collective-permute-start.8
  1337.0 3.4 collective-permute-start.9
  1340.4 5.5 collective-permute-start.10
  1341.7 4.9 collective-permute-start.11
  (77 other events, 457.7 us)
Sparse Core Ops, SparseCore 0:
  1022.4 68.3 all-gather.3
where the time goes:
time: 1370 us; the launch traced here: 1360 us
  local copies, waits for them, and re-layouts  496 us (36%)
  other arithmetic  307 us (22%)
  blocking collectives  255 us (19%)
  matrix products  201 us (15%)
  loops' own time  45.3 us (3%)
  starting transfers between devices  33.5 us (2%)
  between operations  15.7 us (1%)
    gather x3, local copies, waits for them, and re-layouts, per_device(): mobility[k].reshape(-1)[local_index]  241 us
    scatter-add x3, other arithmetic, per_device(): source = jnp.zeros((cell_count,), jnp.float32).at[local_index].add(phase_...  173 us
    dot_general x24, matrix products, one_step(): image = jnp.dot(matrix, search, precision=precise)  138 us
    unnamed x2, blocking collectives  135 us
    gather x2, local copies, waits for them, and re-layouts, per_device(): live_mask.reshape(-1)[local_index]  81.3 us
    gather x2, local copies, waits for them, and re-layouts, per_device(): perf_press = pressure.reshape(-1)[local_index]  81.3 us
    gather x1, local copies, waits for them, and re-layouts, per_device(): total_mob.reshape(-1)[local_index]  80.5 us
    all_gather x1, blocking collectives, per_device(): cells_all = lax.all_gather(well_cells, ('gx', 'gy'), axis=0, tiled=True)  60.6 us
  transfers between devices with their start and end apart: 13, of which 3 were waited for; matrix products, arithmetic and copies ran while one was open for 56% of the time, Pallas kernels for 0%

commit v1 on v0

v1 whole, which is shorter than its diff:
```python
import jax
import jax.numpy as jnp
from jax import lax
from jax.experimental import pallas as pl
from jax.experimental.pallas import tpu as pltpu
from jax.sharding import PartitionSpec as P

CX, CY, NZ = 32, 32, 128
PERF = 16
GROUPS = 8
CITERS = 24
NGX, NGY = 8, 16
NDEV = NGX * NGY
ROWS = 384
RHS_AT, OUT_AT = 320, 328

precise = lax.Precision.HIGHEST
compress = (0.001, 0.001, 0.005)
viscosity = (0.5, 1.5, 0.2)
density = (1.0, 0.8, 0.2)
gravity_step = 0.05
relax = 0.6
dead_leak = 0.001

BIG = 60 * 1024 * 1024
f32, i32 = jnp.float32, jnp.int32
MESH = pl.DeviceIdType.MESH
ANY = pl.BlockSpec(memory_space=pl.ANY)
VMEM = pl.BlockSpec(memory_space=pltpu.VMEM)
SMEM = pl.BlockSpec(memory_space=pltpu.SMEM)


def iota(shape, dim):
    return lax.broadcasted_iota(i32, shape, dim)


def greet(barrier):
    place_x, place_y = lax.axis_index("gx"), lax.axis_index("gy")
    for k in range(1, NGX):
        pl.semaphore_signal(barrier, inc=1, device_id=(lax.rem(place_x + k, NGX), place_y), device_id_type=MESH)
    for k in range(1, NGY):
        pl.semaphore_signal(barrier, inc=1, device_id=(place_x, lax.rem(place_y + k, NGY)), device_id_type=MESH)


def remote(src, dst, send, recv, x, y):
    return pltpu.make_async_remote_copy(
        src_ref=src, dst_ref=dst, send_sem=send, recv_sem=recv, device_id=(x, y), device_id_type=MESH
    )


def exchange_kernel(
    p, ws, gs, act, tx, ty, agg, cells, windex, hole,
    xlo_f, xlo_i, xhi_f, xhi_i, ylo_f, ylo_i, yhi_f, yhi_i, wells,
    face_send, face_recv, send_x, recv_x, send_y, recv_y,
):
    place_x, place_y = lax.axis_index("gx"), lax.axis_index("gy")
    me = place_y * NGX + place_x
    barrier = pltpu.get_barrier_semaphore()
    greet(barrier)
    lane = iota((1, NZ), 1)
    pad = lambda v: jnp.concatenate([v, jnp.zeros((4, NZ - PERF), f32)], axis=1)
    both = pad(cells[...].astype(f32)) + pltpu.roll(pad(windex[...]), PERF, 1)
    row, hole_row = jnp.zeros((1, NZ), f32), jnp.zeros((1, NZ), f32)
    for j in range(4):
        piece = both[j : j + 1]
        if j:
            piece = pltpu.roll(piece, 32 * j, 1)
        row = row + piece
        hole_row = jnp.where(lane // 32 == j, hole[j], hole_row)
    wells[0, pl.ds(me, 1), :] = row
    wells[1, pl.ds(me, 1), :] = hole_row
    pl.semaphore_wait(barrier, NGX - 1 + NGY - 1)

    own = wells.at[:, pl.ds(me, 1), :]
    sends = []
    for k in range(1, NGX):
        sends.append(remote(own, own, send_x.at[k], recv_x.at[k], lax.rem(place_x + k, NGX), place_y))
    up_x, down_x = lax.rem(place_x + 1, NGX), lax.rem(place_x + NGX - 1, NGX)
    up_y, down_y = lax.rem(place_y + 1, NGY), lax.rem(place_y + NGY - 1, NGY)
    faces = []

    def face(src, dst, x, y):
        n = len(faces)
        faces.append(remote(src, dst, face_send.at[n], face_recv.at[n], x, y))

    for n, ref in enumerate((p, ws, gs, tx)):
        face(ref.at[CX - 1], xlo_f.at[n], up_x, place_y)
    for n, ref in enumerate((act, agg)):
        face(ref.at[CX - 1], xlo_i.at[n], up_x, place_y)
    for n, ref in enumerate((p, ws, gs)):
        face(ref.at[0], xhi_f.at[n], down_x, place_y)
    for n, ref in enumerate((act, agg)):
        face(ref.at[0], xhi_i.at[n], down_x, place_y)
    for n, ref in enumerate((p, ws, gs, ty)):
        face(ref.at[:, CY - 1, :], ylo_f.at[n], place_x, up_y)
    for n, ref in enumerate((act, agg)):
        face(ref.at[:, CY - 1, :], ylo_i.at[n], place_x, up_y)
    for n, ref in enumerate((p, ws, gs)):
        face(ref.at[:, 0, :], yhi_f.at[n], place_x, down_y)
    for n, ref in enumerate((act, agg)):
        face(ref.at[:, 0, :], yhi_i.at[n], place_x, down_y)
    for copy in sends + faces:
        copy.start()
    for k in range(1, NGX):
        source = place_y * NGX + lax.rem(place_x + NGX - k, NGX)
        there = wells.at[:, pl.ds(source, 1), :]
        remote(there, there, send_x.at[k], recv_x.at[k], place_x, place_y).wait_recv()
    block = wells.at[:, pl.ds(place_y * NGX, NGX), :]
    for k in range(1, NGY):
        copy = remote(block, block, send_y.at[k], recv_y.at[k], place_x, lax.rem(place_y + k, NGY))
        copy.start()
        sends.append(copy)
    for k in range(1, NGY):
        source = lax.rem(place_y + NGY - k, NGY)
        there = wells.at[:, pl.ds(source * NGX, NGX), :]
        remote(there, there, send_y.at[k], recv_y.at[k], place_x, place_y).wait_recv()
    for copy in faces:
        copy.wait_recv()
    for copy in sends + faces:
        copy.wait_send()


def exchange(p, ws, gs, act, tx, ty, agg, cells, windex, hole):
    shape = lambda n, t: jax.ShapeDtypeStruct((n, 32, NZ), t)
    dma = pltpu.SemaphoreType.DMA
    return pl.pallas_call(
        exchange_kernel,
        out_shape=[
            shape(4, f32), shape(2, i32), shape(3, f32), shape(2, i32),
            shape(4, f32), shape(2, i32), shape(3, f32), shape(2, i32),
            jax.ShapeDtypeStruct((2, NDEV, NZ), f32),
        ],
        in_specs=[ANY] * 7 + [VMEM, VMEM, SMEM],
        out_specs=[ANY] * 8 + [VMEM],
        scratch_shapes=[dma((22,)), dma((22,)), dma((NGX,)), dma((NGX,)), dma((NGY,)), dma((NGY,))],
        compiler_params=pltpu.CompilerParams(collective_id=0, has_side_effects=True, vmem_limit_bytes=BIG),
        name="exchange",
    )(p, ws, gs, act, tx, ty, agg, cells, windex, hole)


def mobility_of(p, ws, gs):
    so = 1.0 - ws - gs
    out = []
    for k, s in enumerate((ws, so, gs)):
        out.append((1.0 + compress[k] * (p - 1.0)) * s * s * (1.0 / viscosity[k]))
    return out


def lane_next(v):
    return pltpu.roll(v, NZ - 1, 1)


def lane_prev(v):
    return pltpu.roll(v, 1, 1)


PAIRS = [(a, b) for a in range(GROUPS) for b in range(a + 1, GROUPS)]


def local_kernel(
    p_h, ws_h, gs_h, old_h, pv_h, tx_h, ty_h, tz_h, act_h, agg_h,
    xlo_fh, xlo_ih, xhi_fh, xhi_ih, ylo_fh, ylo_ih, yhi_fh, yhi_ih, wells,
    res_o, t_o, dinv_o, cx_o, cy_o, cz_o, sums_o, faces_o, parts_o,
    p, ws, gs, act, agg, old, pv, tx, ty, tz,
    xlo_f, xlo_i, xhi_i, ylo_f, ylo_i, yhi_f, yhi_i,
    lam, live, mob, w0, w1, trows, loc, loc_s,
    fy, cx, cy, cz, s, rem, leak, dinv, res, t, yh, acc, e4, own4, nb4, s4,
    sem, out_sem, one_sem,
):
    place_x, place_y = lax.axis_index("gx"), lax.axis_index("gy")
    copies = []

    def fetch(src, dst):
        copy = pltpu.make_async_copy(src, dst, sem.at[len(copies)])
        copy.start()
        copies.append(copy)

    body = (pl.ds(0, CX), pl.ds(0, CY), slice(None))
    for src, dst in ((p_h, p), (ws_h, ws), (gs_h, gs), (act_h, act)):
        fetch(src, dst.at[body])
    for n, dst in enumerate((p, ws, gs)):
        fetch(xhi_fh.at[n], dst.at[CX, pl.ds(0, CY), :])
    fetch(xhi_ih.at[0], act.at[CX, pl.ds(0, CY), :])
    early = len(copies)
    for src, dst in ((xlo_fh, xlo_f), (xlo_ih, xlo_i), (xhi_ih, xhi_i), (ylo_fh, ylo_f), (ylo_ih, ylo_i), (yhi_fh, yhi_f), (yhi_ih, yhi_i)):
        fetch(src, dst)
    for src, dst in ((tx_h, tx), (ty_h, ty), (tz_h, tz), (pv_h, pv), (old_h, old)):
        fetch(src, dst)
    fetch(agg_h, agg.at[body])
    fetch(xhi_ih.at[1], agg.at[CX, pl.ds(0, CY), :])

    lane = iota((NDEV, NZ), 1)
    table = wells[0]
    cell = table.astype(i32)
    cell_x, cell_y, layer = cell >> 16, (cell >> 7) & 511, cell & 127
    slot = lane & 31
    here = (slot < PERF) & (cell >= 0) & ((cell_x >> 5) == place_x) & ((cell_y >> 5) == place_y)
    local = ((((cell_x & 31) << 5) + (cell_y & 31)) << 7) + layer
    local = jnp.where(here, local, -1)
    flag = jnp.where(here, 1.0, 0.0).astype(jnp.bfloat16)
    at_in, at_out = iota((NZ, NZ), 0), iota((NZ, NZ), 1)
    pick = ((at_in // 32 == at_out // 32) & (at_out % 32 == 16)) | (at_out == 17)
    counts = jnp.dot(flag, jnp.where(pick, 1.0, 0.0).astype(jnp.bfloat16), preferred_element_type=f32).astype(i32)
    first_layer = pltpu.roll(layer, 18, 1)
    loc[...] = jnp.where(slot < PERF, local, jnp.where(slot == 18, first_layer, counts))
    to_scalar = pltpu.make_async_copy(loc, loc_s, one_sem)
    to_scalar.start()

    w0[...] = jnp.zeros_like(w0)
    w1[...] = jnp.zeros_like(w1)
    trows[...] = jnp.zeros_like(trows)
    for copy in copies[:early]:
        copy.wait()

    end_x = jnp.where(place_x == NGX - 1, 0.0, 1.0)
    end_y = jnp.where(place_y == NGY - 1, 0.0, 1.0)

    def mobilities(x, _):
        pp = p[x, pl.ds(0, CY), :]
        parts = mobility_of(pp, ws[x, pl.ds(0, CY), :], gs[x, pl.ds(0, CY), :])
        for k in range(3):
            lam[k, x, pl.ds(0, CY), :] = parts[k]
        m = act[x, pl.ds(0, CY), :].astype(f32) * jnp.where(x == CX, end_x, 1.0)
        live[x, pl.ds(0, CY), :] = m
        mob[x] = m * (parts[0] + parts[1] + parts[2])
        return 0

    lax.fori_loop(0, CX + 1, mobilities, 0)
    to_scalar.wait()

    row_lane = iota((1, NZ), 1)

    def one_row(r, _):
        @pl.when(loc_s[r, 17] > 0)
        def _():
            for j in range(4):

                @pl.when(loc_s[r, 32 * j + 16] > 0)
                def _():
                    shift = loc_s[r, 32 * j + 18] - (32 * j + PERF) + 2 * NZ
                    shift = lax.rem(shift, NZ)
                    index_z = pltpu.roll(wells[0, pl.ds(r, 1), :], shift, 1)
                    hole_z = pltpu.roll(wells[1, pl.ds(r, 1), :], shift, 1)
                    drive_z = index_z * hole_z
                    mob_z = jnp.zeros((1, NZ), f32)
                    press_z = jnp.zeros((1, NZ), f32)
                    for k in range(PERF):
                        at = loc_s[r, 32 * j + k]
                        z = (at & 127) | (at >> 31)
                        q = jnp.maximum(at, 0) >> 7
                        qx, qy = q >> 5, q & 31
                        hit = row_lane == z
                        w0[qx, pl.ds(qy, 1), :] += jnp.where(hit, index_z, 0.0)
                        w1[qx, pl.ds(qy, 1), :] += jnp.where(hit, drive_z, 0.0)
                        mob_z = jnp.where(hit, mob[qx, pl.ds(qy, 1), :], mob_z)
                        press_z = jnp.where(hit, p[qx, pl.ds(qy, 1), :], press_z)
                    well = ((r & (NGX - 1)) * NGY + (r >> 3)) * 4 + j
                    trows[pl.ds(well, 1), :] = index_z * mob_z * (hole_z - press_z)

        return 0

    lax.fori_loop(0, NDEV, one_row, 0)
    total = lax.dot_general(
        jnp.ones((8, NZ), f32), trows[...], (((1,), (1,)), ((), ())), precision=precise, preferred_element_type=f32
    )
    sub = iota((8, NZ), 0)
    parts = jnp.zeros((8, NZ), f32)
    for k in range(NGX):
        piece = total[:, NZ * (k // 2) : NZ * (k // 2) + NZ]
        if k % 2:
            piece = pltpu.roll(piece, 64, 1)
        parts = jnp.where(sub == k, piece, parts)
    parts_o[...] = parts

    for copy in copies[early:]:
        copy.wait()

    dead_x = jnp.where(place_x == 0, 0.0, 1.0)
    dead_y = jnp.where(place_y == 0, 0.0, 1.0)
    low = mobility_of(xlo_f[0], xlo_f[1], xlo_f[2])
    face = xlo_f[3] * (xlo_i[0].astype(f32) * dead_x) * live[0, pl.ds(0, CY), :]
    drop = xlo_f[0] - p[0, pl.ds(0, CY), :]
    high = [lam[k, 0, pl.ds(0, CY), :] for k in range(3)]
    below = [face * (0.5 * (low[k] + high[k])) * drop for k in range(3)]
    below.append(face * (0.5 * ((low[0] + low[1] + low[2]) + (high[0] + high[1] + high[2]))))
    cx[0] = below[3]
    low = mobility_of(ylo_f[0], ylo_f[1], ylo_f[2])
    for k in range(3):
        yh[k] = low[k]
    yh[3] = ylo_f[0]
    yh[4] = ylo_f[3] * (ylo_i[0].astype(f32) * dead_y)
    high = mobility_of(yhi_f[0], yhi_f[1], yhi_f[2])
    for k in range(3):
        yh[5 + k] = high[k]
    yh[8] = yhi_f[0]
    yh[9] = yhi_i[0].astype(f32) * end_y

    layer_8 = iota((8, NZ), 1)
    row_8 = iota((8, NZ), 0)

    def residuals(x, carry):
        below = [list(v) for v in carry]
        one = pl.ds(x, 1)
        for k in range(3):
            lam[k, x, pl.ds(CY, 1), :] = yh[5 + k, one, :]
        p[x, pl.ds(CY, 1), :] = yh[8, one, :]
        live[x, pl.ds(CY, 1), :] = yh[9, one, :]
        agg[x, pl.ds(CY, 1), :] = yhi_i[1, one, :]
        own4[2, one, :] = agg[x, pl.ds(0, 1), :]
        own4[3, one, :] = agg[x, pl.ds(CY - 1, 1), :]
        face0 = yh[4, one, :] * live[x, pl.ds(0, 1), :]
        drop0 = yh[3, one, :] - p[x, pl.ds(0, 1), :]
        up0 = [lam[k, x, pl.ds(0, 1), :] for k in range(3)]
        dn0 = [yh[k, one, :] for k in range(3)]
        for k in range(3):
            fy[k, x, pl.ds(0, 1), :] = face0 * (0.5 * (dn0[k] + up0[k])) * drop0
        cy0 = face0 * (0.5 * ((dn0[0] + dn0[1] + dn0[2]) + (up0[0] + up0[1] + up0[2])))
        cy[x, pl.ds(0, 1), :] = cy0
        e4[2, one, :] = cy0
        for c in range(4):
            at = pl.ds(8 * c, 8)
            up = pl.ds(8 * c + 1, 8)
            pp, m = p[x, at, :], live[x, at, :]
            la = [lam[k, x, at, :] for k in range(3)]
            lt = la[0] + la[1] + la[2]
            net = []
            ln = [lam[k, x + 1, at, :] for k in range(3)]
            f = tx[x, at, :] * m * live[x + 1, at, :]
            d = pp - p[x + 1, at, :]
            for k in range(3):
                flux = f * (0.5 * (la[k] + ln[k])) * d
                net.append(flux - below[k][c])
                below[k][c] = flux
            e = f * (0.5 * (lt + (ln[0] + ln[1] + ln[2])))
            cx[x + 1, at, :] = e
            diag = e + below[3][c]
            below[3][c] = e
            ln = [lam[k, x, up, :] for k in range(3)]
            f = ty[x, at, :] * m * live[x, up, :]
            d = pp - p[x, up, :]
            for k in range(3):
                flux = f * (0.5 * (la[k] + ln[k])) * d
                fy[k, x, up, :] = flux
                net[k] = net[k] + (flux - fy[k, x, at, :])
            e = f * (0.5 * (lt + (ln[0] + ln[1] + ln[2])))
            cy[x, up, :] = e
            diag = diag + (e + cy[x, at, :])
            ln = [lane_next(v) for v in la]
            f = jnp.where(layer_8 == NZ - 1, 0.0, tz[x, at, :] * m * lane_next(m))
            d = pp - lane_next(pp)
            for k in range(3):
                flux = f * (0.5 * (la[k] + ln[k])) * (d + density[k] * gravity_step)
                net[k] = net[k] + (flux - lane_prev(flux))
            e = f * (0.5 * (lt + (ln[0] + ln[1] + ln[2])))
            cz[x, at, :] = e
            diag = diag + (e + lane_prev(e))
            sw, sg = ws[x, at, :], gs[x, at, :]
            so = 1.0 - sw - sg
            vol = pv[x, at, :]
            wa, wb = w0[x, at, :], w1[x, at, :]
            pull = m * (wb - pp * wa)
            rhs = None
            for k, sat in enumerate((sw, so, sg)):
                held = (1.0 + compress[k] * (pp - 1.0)) * sat
                r = m * (vol * (held - old[k, x, at, :]) + net[k]) - pull * la[k]
                res[k, x, at, :] = r
                rhs = r if rhs is None else rhs + r
            rhs = -rhs
            store = vol * (compress[0] * sw + compress[1] * so + compress[2] * sg)
            lk = m * (store + m * wa * lt) + dead_leak * (1.0 - m)
            leak[x, at, :] = lk
            diag = diag + lk
            di = relax / diag
            dinv[x, at, :] = di
            sm = rhs * di
            s[x + 1, pl.ds(8 * c + 1, 8), :] = sm
            rem[x, at, :] = rhs - diag * sm
        e4[3, one, :] = cy[x, pl.ds(CY, 1), :]
        s4[2, one, :] = s[x + 1, pl.ds(1, 1), :]
        s4[3, one, :] = s[x + 1, pl.ds(CY, 1), :]
        s[x + 1, pl.ds(0, 1), :] = jnp.zeros((1, NZ), f32)
        s[x + 1, pl.ds(CY + 1, 1), :] = jnp.zeros((1, NZ), f32)
        return tuple(tuple(v) for v in below)

    lax.fori_loop(0, CX, residuals, tuple(tuple(v[8 * c : 8 * c + 8] for c in range(4)) for v in below))
    s4[0] = s[1, pl.ds(1, CY), :]
    s4[1] = s[CX, pl.ds(1, CY), :]
    s[0] = jnp.zeros_like(s[0])
    s[CX + 1] = jnp.zeros_like(s[0])
    outs = []

    def give(src, dst):
        copy = pltpu.make_async_copy(src, dst, out_sem.at[len(outs)])
        copy.start()
        outs.append(copy)

    give(res, res_o)
    give(dinv, dinv_o)
    give(cx, cx_o)
    give(cy, cy_o)
    give(cz, cz_o)
    give(s4, faces_o)

    zero = jnp.zeros((8, NZ), f32)

    def remainders(x, carry):
        lk_sum, re_sum, z_sum = [list(v) for v in carry]
        for c in range(4):
            at = pl.ds(8 * c, 8)
            up = pl.ds(8 * c + 1, 8)
            here = s[x + 1, up, :]
            z = cz[x, at, :]
            near = cx[x + 1, at, :] * s[x + 2, up, :] + cx[x, at, :] * s[x, up, :]
            near = near + (cy[x, up, :] * s[x + 1, pl.ds(8 * c + 2, 8), :] + cy[x, at, :] * s[x + 1, at, :])
            near = near + (z * lane_next(here) + lane_prev(z * here))
            re = rem[x, at, :] + near
            t[x, at, :] = here + dinv[x, at, :] * re
            lk = leak[x, at, :]
            a = agg[x, at, :]
            cross = jnp.where(a != lane_next(a), z, 0.0)
            for g in range(GROUPS):
                hit = a == g
                re_sum[g] = re_sum[g] + jnp.where(hit, re, 0.0)
                lk_sum[g] = lk_sum[g] + jnp.where(hit, lk, 0.0)
                if g < GROUPS - 1:
                    z_sum[g] = z_sum[g] + jnp.where(hit, cross, 0.0)
        return tuple(lk_sum), tuple(re_sum), tuple(z_sum)

    lk_sum, re_sum, z_sum = lax.fori_loop(
        0, CX, remainders, ((zero,) * GROUPS, (zero,) * GROUPS, (zero,) * (GROUPS - 1))
    )
    give(t, t_o)

    def line(v):
        return jnp.sum(v, axis=0, keepdims=True)

    acc[...] = jnp.zeros_like(acc)
    for g in range(GROUPS):
        acc[g * GROUPS + g, :] = line(lk_sum[g])[0]
        acc[RHS_AT + g, :] = line(re_sum[g])[0]

    def crossings(x, sums):
        sums = list(sums)
        for c in range(4):
            at = pl.ds(8 * c, 8)
            up = pl.ds(8 * c + 1, 8)
            a = agg[x, at, :]
            for b, e, ok in (
                (agg[x + 1, at, :], cx[x + 1, at, :], x < CX - 1),
                (agg[x, up, :], cy[x, up, :], (row_8 < 7) if c == 3 else None),
            ):
                code = jnp.minimum(a, b) * GROUPS + jnp.maximum(a, b)
                if ok is not None:
                    code = jnp.where(ok, code, -1)
                for n, (g, h) in enumerate(PAIRS):
                    sums[n] = sums[n] + jnp.where(code == g * GROUPS + h, e, 0.0)
        return tuple(sums)

    sums = lax.fori_loop(0, CX, crossings, (zero,) * len(PAIRS))
    for n, (g, h) in enumerate(PAIRS):
        v = sums[n]
        if h == g + 1:
            v = v + z_sum[g]
        v = line(v)[0]
        acc[h * GROUPS + g, :] = v
        acc[g * GROUPS + h, :] = v

    e4[0] = cx[0]
    e4[1] = cx[CX]
    own4[0] = agg[0, pl.ds(0, CY), :]
    own4[1] = agg[CX - 1, pl.ds(0, CY), :]
    nb4[0] = xlo_i[1]
    nb4[1] = xhi_i[1]
    nb4[2] = ylo_i[1]
    nb4[3] = yhi_i[1]

    def side(d, _):
        e, a, b = e4[d], own4[d], nb4[d]
        es = e * s4[d]
        goes = []
        for g in range(GROUPS):
            goes.append(line(jnp.where(b == g, es, 0.0)))
        acc[pl.ds(pl.multiple_of(OUT_AT + d * GROUPS, 8), GROUPS), :] = jnp.concatenate(goes, axis=0)
        for h in range(GROUPS):
            w = jnp.where(b == h, e, 0.0)
            rows = [line(jnp.where(a == g, w, 0.0)) for g in range(GROUPS)]
            start = pl.multiple_of(((d + 1) * GROUPS + h) * GROUPS, 8)
            acc[pl.ds(start, GROUPS), :] = jnp.concatenate(rows, axis=0)
        return 0

    lax.fori_loop(0, 4, side, 0)
    for n in range(3):
        flat = jnp.sum(acc[pl.ds(NZ * n, NZ), :].T, axis=0, keepdims=True)
        sums_o[n] = flat
    for copy in outs:
        copy.wait()


def local(args, halos, wells):
    v = pltpu.VMEM
    blk = (CX, CY, NZ)
    sds = jax.ShapeDtypeStruct
    dma = pltpu.SemaphoreType.DMA
    return pl.pallas_call(
        local_kernel,
        out_shape=[
            sds((3,) + blk, f32), sds(blk, f32), sds(blk, f32), sds((CX + 1, CY, NZ), f32),
            sds((CX, CY + 8, NZ), f32), sds(blk, f32), sds((3, 1, NZ), f32), sds((4, 32, NZ), f32), sds((8, NZ), f32),
        ],
        in_specs=[ANY] * 18 + [VMEM],
        out_specs=[ANY] * 6 + [VMEM, ANY, VMEM],
        scratch_shapes=[
            v((CX + 1, CY + 8, NZ), f32), v((CX + 1, CY, NZ), f32), v((CX + 1, CY, NZ), f32), v((CX + 1, CY, NZ), i32),
            v((CX + 1, CY + 8, NZ), i32), v((3,) + blk, f32), v(blk, f32), v(blk, f32), v(blk, f32), v(blk, f32),
            v((4, 32, NZ), f32), v((2, 32, NZ), i32), v((2, 32, NZ), i32), v((4, 32, NZ), f32), v((2, 32, NZ), i32),
            v((3, 32, NZ), f32), v((2, 32, NZ), i32),
            v((3, CX + 1, CY + 8, NZ), f32), v((CX + 1, CY + 8, NZ), f32), v((CX + 1, CY, NZ), f32),
            v(blk, f32), v(blk, f32), v((4 * NDEV, NZ), f32), v((NDEV, NZ), i32), pltpu.SMEM((NDEV, NZ), i32),
            v((3, CX, CY + 8, NZ), f32), v((CX + 1, CY, NZ), f32), v((CX, CY + 8, NZ), f32), v(blk, f32),
            v((CX + 2, CY + 8, NZ), f32), v(blk, f32), v(blk, f32), v(blk, f32), v((3,) + blk, f32), v(blk, f32),
            v((10, 32, NZ), f32), v((ROWS, NZ), f32), v((4, 32, NZ), f32), v((4, 32, NZ), i32), v((4, 32, NZ), i32), v((4, 32, NZ), f32),
            dma((32,)), dma((8,)), dma,
        ],
        compiler_params=pltpu.CompilerParams(vmem_limit_bytes=BIG),
        name="local",
    )(*args, *halos, wells)


def coarse_kernel(
    sums, parts, faces, t_h, dinv_h, cx_h, cy_h, cz_h, agg_h, xlo_i, xhi_i, ylo_i, yhi_i,
    update_o, well_o,
    gather, mat, slots, send_rows, rows_x, rows_y, tall, dinv, cx, cy, cz, agg, far, pc,
    sem, send_x, recv_x, send_y, recv_y, psend_x, precv_x, psend_y, precv_y, fsend, frecv,
):
    place_x, place_y = lax.axis_index("gx"), lax.axis_index("gy")
    me = place_y * NGX + place_x
    barrier = pltpu.get_barrier_semaphore()
    greet(barrier)
    loads = []
    body = (slice(None), pl.ds(0, CY), slice(None))
    for src, dst in ((t_h, tall), (dinv_h, dinv), (cx_h, cx), (cy_h, cy), (cz_h, cz), (agg_h, agg)):
        copy = pltpu.make_async_copy(src, dst, sem.at[len(loads)])
        copy.start()
        loads.append(copy)
    for n in range(3):
        gather[n, pl.ds(me, 1), :] = sums[n]
    rows_x[pl.ds(place_x, 1), :] = parts[pl.ds(place_x, 1), :]
    pl.semaphore_wait(barrier, NGX - 1 + NGY - 1)

    sends = []
    own = gather.at[:, pl.ds(me, 1), :]
    for k in range(1, NGX):
        peer = lax.rem(place_x + k, NGX)
        sends.append(remote(own, own, send_x.at[k], recv_x.at[k], peer, place_y))
    for k in range(1, NGX):
        peer = lax.rem(place_x + k, NGX)
        sends.append(
            remote(parts.at[pl.ds(peer, 1), :], rows_x.at[pl.ds(place_x, 1), :], psend_x.at[k], precv_x.at[k], peer, place_y)
        )
    halo = [
        remote(faces.at[1], far.at[0], fsend.at[0], frecv.at[0], lax.rem(place_x + 1, NGX), place_y),
        remote(faces.at[0], far.at[1], fsend.at[1], frecv.at[1], lax.rem(place_x + NGX - 1, NGX), place_y),
        remote(faces.at[3], far.at[2], fsend.at[2], frecv.at[2], place_x, lax.rem(place_y + 1, NGY)),
        remote(faces.at[2], far.at[3], fsend.at[3], frecv.at[3], place_x, lax.rem(place_y + NGY - 1, NGY)),
    ]
    for copy in sends + halo:
        copy.start()
    for k in range(1, NGX):
        source = place_y * NGX + lax.rem(place_x + NGX - k, NGX)
        there = gather.at[:, pl.ds(source, 1), :]
        remote(there, there, send_x.at[k], recv_x.at[k], place_x, place_y).wait_recv()
    block = gather.at[:, pl.ds(place_y * NGX, NGX), :]
    for k in range(1, NGY):
        copy = remote(block, block, send_y.at[k], recv_y.at[k], place_x, lax.rem(place_y + k, NGY))
        copy.start()
        sends.append(copy)
    for k in range(1, NGX):
        source = lax.rem(place_x + NGX - k, NGX)
        there = rows_x.at[pl.ds(source, 1), :]
        remote(there, there, psend_x.at[k], precv_x.at[k], place_x, place_y).wait_recv()
    line = jnp.sum(rows_x[...], axis=0, keepdims=True)
    for k in range(NGY):
        send_rows[k : k + 1, :] = line if k == 0 else pltpu.roll(line, NZ - 4 * k, 1)
    rows_y[pl.ds(place_y, 1), :] = send_rows[pl.ds(place_y, 1), :]
    for k in range(1, NGY):
        peer = lax.rem(place_y + k, NGY)
        copy = remote(
            send_rows.at[pl.ds(peer, 1), :], rows_y.at[pl.ds(place_y, 1), :], psend_y.at[k], precv_y.at[k], place_x, peer
        )
        copy.start()
        sends.append(copy)
    for k in range(1, NGY):
        source = lax.rem(place_y + NGY - k, NGY)
        there = gather.at[:, pl.ds(source * NGX, NGX), :]
        remote(there, there, send_y.at[k], recv_y.at[k], place_x, place_y).wait_recv()

    for n in range(3):
        mat[pl.ds(NZ * n, NZ), :] = gather[n].T
    sub = iota((8, NZ), 0)

    def rows(n):
        return mat[pl.ds(8 * n, 8), :]

    moves = (0, 1, NZ - 1, NGX, NZ - NGX)
    total = jnp.zeros((8, NZ), f32)
    for n in range(5 * GROUPS):
        total = total + rows(n)
    for h in range(GROUPS):
        block = rows(h)
        slots[pl.ds(8 * h, 8), :] = jnp.where(sub == h, total, -block)
    for d in range(1, 5):
        for h in range(GROUPS):
            v = -rows(d * GROUPS + h)
            slots[pl.ds((d * GROUPS + h) * 8, 8), :] = pltpu.roll(v, (NZ - moves[d]) % NZ, 1)
    rhs = rows(RHS_AT // 8)
    for d in range(1, 5):
        away = (0, 2, 1, 4, 3)[d]
        rhs = rhs + pltpu.roll(rows(OUT_AT // 8 + away - 1), moves[d], 1)

    def dot(a, b):
        return jnp.sum(jnp.sum(a * b, axis=0, keepdims=True), axis=1, keepdims=True)

    def one_step(_, carry):
        x, r, q, rr = carry
        sums5 = [None] * 5
        for h in range(GROUPS):
            spread = jnp.broadcast_to(q[h : h + 1, :], (8, NZ))
            for d in range(5):
                v = slots[pl.ds((d * GROUPS + h) * 8, 8), :] * spread
                sums5[d] = v if sums5[d] is None else sums5[d] + v
        image = sums5[0]
        for d in range(1, 5):
            image = image + pltpu.roll(sums5[d], moves[d], 1)
        alpha = rr / dot(q, image)
        x = x + alpha * q
        r = r - alpha * image
        new = dot(r, r)
        q = r + (new / rr) * q
        return x, r, q, new

    coarse = lax.fori_loop(0, CITERS, one_step, (jnp.zeros((8, NZ), f32), rhs, rhs, dot(rhs, rhs)))[0]
    mine = iota((8, NZ), 1) == me
    values = []
    for d in range(5):
        v = coarse if d == 0 else pltpu.roll(coarse, moves[d], 1)
        values.append(jnp.sum(jnp.where(mine, v, 0.0), axis=1, keepdims=True))

    def look_up(ids, d):
        v = jnp.broadcast_to(values[d][0:1, :], ids.shape)
        for g in range(1, GROUPS):
            v = jnp.where(ids == g, values[d][g : g + 1, :], v)
        return v

    for copy in halo:
        copy.wait_recv()
    for copy in loads:
        copy.wait()
    far[0] = cx[0] * (far[0] + look_up(xlo_i[1], 1))
    far[1] = far[1] + look_up(xhi_i[1], 2)
    far[2] = far[2] + look_up(ylo_i[1], 3)
    far[3] = far[3] + look_up(yhi_i[1], 4)

    def fill(x, _):
        pc[x, pl.ds(0, CY), :] = look_up(agg[x], 0)
        pc[x, pl.ds(CY, 1), :] = far[3, pl.ds(x, 1), :]
        return 0

    lax.fori_loop(0, CX, fill, 0)
    pc[CX, pl.ds(0, CY), :] = far[1]
    def finish(x, below):
        c_here = pc[x, pl.ds(0, CY), :]
        e = cx[x + 1]
        near = e * pc[x + 1, pl.ds(0, CY), :] + below
        above = e * c_here
        up = cy[x, pl.ds(1, CY), :]
        near = near + up * pc[x, pl.ds(1, CY), :]
        lowrow = cy[x, pl.ds(0, 1), :] * far[2, pl.ds(x, 1), :]
        down = pltpu.roll(up * c_here, 1, 0)
        near = near + jnp.where(iota((CY, NZ), 0) == 0, lowrow, down)
        z = cz[x]
        near = near + (z * lane_next(c_here) + lane_prev(z * c_here))
        update_o[x] = tall[x] + (1.0 - relax) * c_here + dinv[x] * near
        return above

    lax.fori_loop(0, CX, finish, far[0])
    for k in range(1, NGY):
        source = lax.rem(place_y + NGY - k, NGY)
        there = rows_y.at[pl.ds(source, 1), :]
        remote(there, there, psend_y.at[k], precv_y.at[k], place_x, place_y).wait_recv()
    well_o[...] = jnp.sum(rows_y[...], axis=0, keepdims=True)
    for copy in sends + halo:
        copy.wait_send()


def coarse_part(sums, parts, faces, t, dinv, cx, cy, cz, agg, xlo_i, xhi_i, ylo_i, yhi_i):
    v = pltpu.VMEM
    blk = (CX, CY, NZ)
    sds = jax.ShapeDtypeStruct
    dma = pltpu.SemaphoreType.DMA
    return pl.pallas_call(
        coarse_kernel,
        out_shape=[sds(blk, f32), sds((1, NZ), f32)],
        in_specs=[VMEM, VMEM, ANY] + [ANY] * 6 + [VMEM] * 4,
        out_specs=[VMEM, VMEM],
        scratch_shapes=[
            v((3, NDEV, NZ), f32), v((ROWS, NZ), f32), v((5 * 64, NZ), f32), v((NGY, NZ), f32), v((NGX, NZ), f32), v((NGY, NZ), f32),
            v(blk, f32), v(blk, f32), v((CX + 1, CY, NZ), f32), v((CX, CY + 8, NZ), f32), v(blk, f32), v(blk, i32),
            v((4, 32, NZ), f32), v((CX + 1, CY + 8, NZ), f32),
            dma((8,)), dma((NGX,)), dma((NGX,)), dma((NGY,)), dma((NGY,)),
            dma((NGX,)), dma((NGX,)), dma((NGY,)), dma((NGY,)), dma((4,)), dma((4,)),
        ],
        compiler_params=pltpu.CompilerParams(
            collective_id=1, has_side_effects=True, vmem_limit_bytes=BIG
        ),
        name="coarse",
    )(sums, parts, faces, t, dinv, cx, cy, cz, agg, xlo_i, xhi_i, ylo_i, yhi_i)


def per_device(
    pressure, water_sat, gas_sat, old_content, pore_volume, trans_x, trans_y, trans_z, active, aggregate,
    well_cells, well_index, bottom_hole, well_target,
):
    *halos, wells = exchange(
        pressure, water_sat, gas_sat, active, trans_x, trans_y, aggregate, well_cells, well_index, bottom_hole
    )
    xlo_f, xlo_i, xhi_f, xhi_i, ylo_f, ylo_i, yhi_f, yhi_i = halos
    args = (pressure, water_sat, gas_sat, old_content, pore_volume, trans_x, trans_y, trans_z, active, aggregate)
    residual, t, dinv, cx, cy, cz, sums, faces, parts = local(args, halos, wells)
    update, well = coarse_part(sums, parts, faces, t, dinv, cx, cy, cz, aggregate, xlo_i, xhi_i, ylo_i, yhi_i)
    return residual, update, well[0, :4] - well_target


def solution(mesh):
    cells = P("gx", "gy", None)
    three = P(None, "gx", "gy", None)
    well, one = P(("gx", "gy"), None), P(("gx", "gy"))
    return jax.shard_map(
        per_device,
        mesh=mesh,
        in_specs=(cells, cells, cells, three) + (cells,) * 6 + (well, well, one, one),
        out_specs=(three, cells, one),
        check_vma=False,
    )
```

time: 1370 us -> 69.1 us (0.05); the launches traced: 1360 us -> 68.8 us
  local copies, waits for them, and re-layouts: 496 us -> 1.87 us
  other arithmetic: 307 us -> 1.19 us
  blocking collectives: 255 us -> 0 us
  matrix products: 201 us -> 0 us
  Pallas kernels: 0 us -> 65.1 us
  loops' own time: 45.3 us -> 0 us
  starting transfers between devices: 33.5 us -> 0 us
  between operations: 15.7 us -> 0.67 us
    gather x8 -> x0, local copies, waits for them, and re-layouts: 484 us -> none  [the longest x3 241 us: per_device(): mobility[k].reshape(-1)[local_index]]
    scatter-add x4 -> x0, other arithmetic: 231 us -> none  [the longest x3 173 us: per_device(): source = jnp.zeros((cell_count,), jnp.float32).at[local_index].add(phase_...]
    dot_general x36 -> x0, matrix products: 201 us -> none  [the longest x24 138 us: one_step(): image = jnp.dot(matrix, search, precision=precise)]
    unnamed x2 -> x0, blocking collectives: 135 us -> none
    all_gather x2 -> x0, blocking collectives: 120 us -> none  [the longest x1 60.6 us: per_device(): cells_all = lax.all_gather(well_cells, ('gx', 'gy'), axis=0, tiled=True)]
    pallas_call x0 -> x3, Pallas kernels: none -> 65.1 us  [the longest x1 25 us: coarse_part(): pl.pallas_call(coarse_kernel, out_shape=[sds(blk, f32), sds((1, NZ), f32)...]
    another operation x1 -> x0, loops' own time: 45.3 us -> none  [coarse_solve(): return lax.fori_loop(0, CITERS, one_step, start)[0]]
    reduce_sum x56 -> x0, other arithmetic: 37.3 us -> none  [the longest x24 16.5 us: one_step(): alpha = norm_now / jnp.sum(search * image)]
  transfers between devices with their start and end apart: 13 -> 0, of which waited for: 3 -> 0; matrix products, arithmetic and copies ran while one was open for 56% -> 0% of each run, Pallas kernels for 0% -> 0%
where the time goes in v1:
time: 69.1 us; the launch traced here: 68.8 us
  Pallas kernels  65.1 us (94%)
  local copies, waits for them, and re-layouts  1.87 us (3%)
  other arithmetic  1.19 us (2%)
    pallas_call x1, Pallas kernels, coarse_part(): pl.pallas_call(coarse_kernel, out_shape=[sds(blk, f32), sds((1, NZ), f32)...  25 us
    pallas_call x1, Pallas kernels, local(): pl.pallas_call(local_kernel, out_shape=[sds((3,) + blk, f32), sds(blk, f3...  21.7 us
    pallas_call x1, Pallas kernels, exchange(): pl.pallas_call(exchange_kernel, out_shape=[shape(4, f32), shape(2, i32),...  18.4 us
    unnamed x3, local copies, waits for them, and re-layouts  1.87 us

profile of v1, /device:TPU:1, one launch (start us, length us, event | category | flops | bytes accessed | tf_op | source)
XLA Modules:
  0.0 68.8 jit_solution(18250801655394575485)
XLA Ops:
  0.6 18.4 %exchange.1 = (f32[4,32,128]{2,1,0:T(8,128)}, s32[2,32,128]{2,1,0:T(8,128)}, f32[3,32,128]{2,1,0:T(8,128)}, s32[2,32,128]{2,1,0:T(8,128)}, f32[4,32,128]{2,1,0:T...) custom-call(f32[32,32,128]{2,1,0:T(8,128)} %p_h.1, ...), custom_call_target="tpu_custom_call" | custom-call | tf_op jit(solution)/shard_map/exchange/pallas_call | solution.py:126
  19.1 21.7 %local.1 = (f32[3,32,32,128]{3,2,1,0:T(8,128)}, f32[32,32,128]{2,1,0:T(8,128)}, f32[32,32,128]{2,1,0:T(8,128)}, f32[33,32,128]{2,1,0:T(8,128)}, f32[32,40,128]{2...) custom-call(f32[32,32,128]{2,1,0:T(8,128)} %p_h.1, ...), custom_call_target="tpu_custom_call" | custom-call | tf_op jit(solution)/shard_map/local/pallas_call | solution.py:504
  40.8 0.0 copy-start
  40.8 25.0 %coarse.1 = (f32[32,32,128]{2,1,0:T(8,128)}, f32[1,128]{1,0:T(1,128)}) custom-call(f32[3,1,128]{2,1,0:T(1,128)} %get-tuple-element.33.sums, f32[8,128]{1,0:T(8,128)} %get-tuple-element.34.parts, f32[4,32,128]{2,1,0:T(8,128)} %get-tuple-element.35.faces, f32[32,32,128]{2,1,0:T(8,128)} %get-tuple-element.36.t_h, f32[32,32,128]{2,1,0:T(8,128)} %get-tuple-element.37.dinv_h, ...), custom_call_target="tpu_custom_call" | custom-call | tf_op jit(solution)/shard_map/coarse/pallas_call | solution.py:700
  65.8 0.0 copy-done
  65.8 1.2 %bitcast_subtract_fusion = f32[4]{0:T(128)} fusion(f32[4]{0:T(128)S(1)} %copy-done, f32[1,128]{1,0:T(1,128)} %get-tuple-element.42), kind=kLoop, calls=%fused_computation | loop fusion | flops 4 | bytes 48 | tf_op jit(solution)/shard_map/sub | solution.py:730
  67.0 1.9 %copy.18 = f32[32,32,128]{2,1,0:T(8,128)} copy(f32[32,32,128]{2,1,0:T(8,128)} %get-tuple-element.47) | data formatting | bytes 1048576
Async XLA Ops:
  40.8 25.0 %copy-start = (f32[4]{0:T(128)S(1)}, f32[4]{0:T(128)}, u32[]{:S(2)}) copy-start(f32[4]{0:T(128)} %param.27) | copy-start | bytes 52

commit v2 on v1

v2 whole, which is shorter than its diff:
```python
import jax
import jax.numpy as jnp
from jax import lax
from jax.experimental import pallas as pl
from jax.experimental.pallas import tpu as pltpu
from jax.sharding import PartitionSpec as P

CX, CY, NZ = 32, 32, 128
PERF = 16
GROUPS = 8
CITERS = 24
NGX, NGY = 8, 16
NDEV = NGX * NGY
ROWS = 384
RHS_AT, OUT_AT, LEAK_AT = 320, 328, 360

precise = lax.Precision.HIGHEST
compress = (0.001, 0.001, 0.005)
viscosity = (0.5, 1.5, 0.2)
density = (1.0, 0.8, 0.2)
gravity_step = 0.05
relax = 0.6
dead_leak = 0.001

BIG = 60 * 1024 * 1024
f32, i32 = jnp.float32, jnp.int32
MESH = pl.DeviceIdType.MESH
ANY = pl.BlockSpec(memory_space=pl.ANY)
VMEM = pl.BlockSpec(memory_space=pltpu.VMEM)
SMEM = pl.BlockSpec(memory_space=pltpu.SMEM)


def iota(shape, dim):
    return lax.broadcasted_iota(i32, shape, dim)


def greet(barrier):
    place_x, place_y = lax.axis_index("gx"), lax.axis_index("gy")
    for k in range(1, NGX):
        pl.semaphore_signal(barrier, inc=1, device_id=(lax.rem(place_x + k, NGX), place_y), device_id_type=MESH)
    for k in range(1, NGY):
        pl.semaphore_signal(barrier, inc=1, device_id=(place_x, lax.rem(place_y + k, NGY)), device_id_type=MESH)


def loop(first, last, body, carry, steps):
    def several(i, carry):
        for n in range(steps):
            carry = body(first + i * steps + n, carry)
        return carry

    return lax.fori_loop(0, (last - first) // steps, several, carry)


def remote(src, dst, send, recv, x, y):
    return pltpu.make_async_remote_copy(
        src_ref=src, dst_ref=dst, send_sem=send, recv_sem=recv, device_id=(x, y), device_id_type=MESH
    )


def mobility_of(p, ws, gs):
    so = 1.0 - ws - gs
    out = []
    for k, s in enumerate((ws, so, gs)):
        out.append((1.0 + compress[k] * (p - 1.0)) * s * s * (1.0 / viscosity[k]))
    return out


def lane_next(v):
    return pltpu.roll(v, NZ - 1, 1)


def lane_prev(v):
    return pltpu.roll(v, 1, 1)


def line(v):
    return jnp.sum(v, axis=0, keepdims=True)


PAIRS = [(a, b) for a in range(GROUPS) for b in range(a + 1, GROUPS)]
BODY = (pl.ds(0, CX), pl.ds(0, CY), slice(None))


def exchange_kernel(
    p_h, ws_h, gs_h, act_h, tx_h, ty_h, tz_h, agg_h, cells, windex, hole,
    net_o, cx_o, cy_o, cz_o, mob_o, sums_o, nb_o, wells,
    p, ws, gs, act, tx, ty, tz, agg, xlo_f, xlo_i, xhi_f, xhi_i, ylo_f, ylo_i, yhi_f, yhi_i,
    lam, live, mob, net, fy, cx, cy, cz, yh, acc, e4, own4, nb4,
    load_sem, out_sem, face_send, face_recv, send_x, recv_x, send_y, recv_y,
):
    place_x, place_y = lax.axis_index("gx"), lax.axis_index("gy")
    me = place_y * NGX + place_x
    barrier = pltpu.get_barrier_semaphore()
    greet(barrier)
    loads = []
    for src, dst in (
        (p_h, p.at[BODY]), (ws_h, ws), (gs_h, gs), (act_h, act), (tx_h, tx), (ty_h, ty), (tz_h, tz), (agg_h, agg.at[BODY])
    ):
        copy = pltpu.make_async_copy(src, dst, load_sem.at[len(loads)])
        copy.start()
        loads.append(copy)
    lane = iota((1, NZ), 1)
    pad = lambda v: jnp.concatenate([v, jnp.zeros((4, NZ - PERF), f32)], axis=1)
    both = pad(cells[...].astype(f32)) + pltpu.roll(pad(windex[...]), PERF, 1)
    row, hole_row = jnp.zeros((1, NZ), f32), jnp.zeros((1, NZ), f32)
    for j in range(4):
        piece = both[j : j + 1]
        if j:
            piece = pltpu.roll(piece, 32 * j, 1)
        row = row + piece
        hole_row = jnp.where(lane // 32 == j, hole[j], hole_row)
    wells[0, pl.ds(me, 1), :] = row
    wells[1, pl.ds(me, 1), :] = hole_row
    pl.semaphore_wait(barrier, NGX - 1 + NGY - 1)

    own = wells.at[:, pl.ds(me, 1), :]
    sends = []
    for k in range(1, NGX):
        sends.append(remote(own, own, send_x.at[k], recv_x.at[k], lax.rem(place_x + k, NGX), place_y))
    up_x, down_x = lax.rem(place_x + 1, NGX), lax.rem(place_x + NGX - 1, NGX)
    up_y, down_y = lax.rem(place_y + 1, NGY), lax.rem(place_y + NGY - 1, NGY)
    faces = []

    def face(src, dst, x, y):
        n = len(faces)
        faces.append(remote(src, dst, face_send.at[n], face_recv.at[n], x, y))

    for n, ref in enumerate((p_h, ws_h, gs_h, tx_h)):
        face(ref.at[CX - 1], xlo_f.at[n], up_x, place_y)
    for n, ref in enumerate((act_h, agg_h)):
        face(ref.at[CX - 1], xlo_i.at[n], up_x, place_y)
    for n, ref in enumerate((p_h, ws_h, gs_h)):
        face(ref.at[0], xhi_f.at[n], down_x, place_y)
    for n, ref in enumerate((act_h, agg_h)):
        face(ref.at[0], xhi_i.at[n], down_x, place_y)
    for n, ref in enumerate((p_h, ws_h, gs_h, ty_h)):
        face(ref.at[:, CY - 1, :], ylo_f.at[n], place_x, up_y)
    for n, ref in enumerate((act_h, agg_h)):
        face(ref.at[:, CY - 1, :], ylo_i.at[n], place_x, up_y)
    for n, ref in enumerate((p_h, ws_h, gs_h)):
        face(ref.at[:, 0, :], yhi_f.at[n], place_x, down_y)
    for n, ref in enumerate((act_h, agg_h)):
        face(ref.at[:, 0, :], yhi_i.at[n], place_x, down_y)
    for copy in sends + faces:
        copy.start()

    for copy in loads[:4]:
        copy.wait()

    def mobilities(x, _):
        parts = mobility_of(p[x, pl.ds(0, CY), :], ws[x], gs[x])
        for k in range(3):
            lam[k, x, pl.ds(0, CY), :] = parts[k]
        m = act[x].astype(f32)
        live[x, pl.ds(0, CY), :] = m
        mob[x] = m * (parts[0] + parts[1] + parts[2])
        return 0

    loop(0, CX, mobilities, 0, 8)
    outs = []

    def give(src, dst):
        copy = pltpu.make_async_copy(src, dst, out_sem.at[len(outs)])
        copy.start()
        outs.append(copy)

    give(mob, mob_o)
    for copy in loads[4:]:
        copy.wait()
    for copy in faces:
        copy.wait_recv()

    end_x = jnp.where(place_x == NGX - 1, 0.0, 1.0)
    end_y = jnp.where(place_y == NGY - 1, 0.0, 1.0)
    dead_x = jnp.where(place_x == 0, 0.0, 1.0)
    dead_y = jnp.where(place_y == 0, 0.0, 1.0)
    high = mobility_of(xhi_f[0], xhi_f[1], xhi_f[2])
    for k in range(3):
        lam[k, CX, pl.ds(0, CY), :] = high[k]
    p[CX, pl.ds(0, CY), :] = xhi_f[0]
    live[CX, pl.ds(0, CY), :] = xhi_i[0].astype(f32) * end_x
    agg[CX, pl.ds(0, CY), :] = xhi_i[1]
    low = mobility_of(xlo_f[0], xlo_f[1], xlo_f[2])
    face_trans = xlo_f[3] * (xlo_i[0].astype(f32) * dead_x) * live[0, pl.ds(0, CY), :]
    drop = xlo_f[0] - p[0, pl.ds(0, CY), :]
    high = [lam[k, 0, pl.ds(0, CY), :] for k in range(3)]
    below = [face_trans * (0.5 * (low[k] + high[k])) * drop for k in range(3)]
    below.append(face_trans * (0.5 * ((low[0] + low[1] + low[2]) + (high[0] + high[1] + high[2]))))
    cx[0] = below[3]
    low = mobility_of(ylo_f[0], ylo_f[1], ylo_f[2])
    for k in range(3):
        yh[k] = low[k]
    yh[3] = ylo_f[0]
    yh[4] = ylo_f[3] * (ylo_i[0].astype(f32) * dead_y)
    high = mobility_of(yhi_f[0], yhi_f[1], yhi_f[2])
    for k in range(3):
        yh[5 + k] = high[k]
    yh[8] = yhi_f[0]
    yh[9] = yhi_i[0].astype(f32) * end_y
    layer_8 = iota((8, NZ), 1)
    row_8 = iota((8, NZ), 0)

    def fluxes(x, carry):
        below = [list(v) for v in carry]
        one = pl.ds(x, 1)
        for k in range(3):
            lam[k, x, pl.ds(CY, 1), :] = yh[5 + k, one, :]
        p[x, pl.ds(CY, 1), :] = yh[8, one, :]
        live[x, pl.ds(CY, 1), :] = yh[9, one, :]
        agg[x, pl.ds(CY, 1), :] = yhi_i[1, one, :]
        own4[2, one, :] = agg[x, pl.ds(0, 1), :]
        own4[3, one, :] = agg[x, pl.ds(CY - 1, 1), :]
        face0 = yh[4, one, :] * live[x, pl.ds(0, 1), :]
        drop0 = yh[3, one, :] - p[x, pl.ds(0, 1), :]
        up0 = [lam[k, x, pl.ds(0, 1), :] for k in range(3)]
        dn0 = [yh[k, one, :] for k in range(3)]
        for k in range(3):
            fy[k, x, pl.ds(0, 1), :] = face0 * (0.5 * (dn0[k] + up0[k])) * drop0
        cy0 = face0 * (0.5 * ((dn0[0] + dn0[1] + dn0[2]) + (up0[0] + up0[1] + up0[2])))
        cy[x, pl.ds(0, 1), :] = cy0
        e4[2, one, :] = cy0
        for c in range(4):
            at = pl.ds(8 * c, 8)
            up = pl.ds(8 * c + 1, 8)
            pp, m = p[x, at, :], live[x, at, :]
            la = [lam[k, x, at, :] for k in range(3)]
            lt = la[0] + la[1] + la[2]
            sums = []
            ln = [lam[k, x + 1, at, :] for k in range(3)]
            f = tx[x, at, :] * m * live[x + 1, at, :]
            d = pp - p[x + 1, at, :]
            for k in range(3):
                flux = f * (0.5 * (la[k] + ln[k])) * d
                sums.append(flux - below[k][c])
                below[k][c] = flux
            e = f * (0.5 * (lt + (ln[0] + ln[1] + ln[2])))
            cx[x + 1, at, :] = e
            ln = [lam[k, x, up, :] for k in range(3)]
            f = ty[x, at, :] * m * live[x, up, :]
            d = pp - p[x, up, :]
            for k in range(3):
                flux = f * (0.5 * (la[k] + ln[k])) * d
                fy[k, x, up, :] = flux
                sums[k] = sums[k] + (flux - fy[k, x, at, :])
            e = f * (0.5 * (lt + (ln[0] + ln[1] + ln[2])))
            cy[x, up, :] = e
            ln = [lane_next(v) for v in la]
            f = jnp.where(layer_8 == NZ - 1, 0.0, tz[x, at, :] * m * lane_next(m))
            d = pp - lane_next(pp)
            for k in range(3):
                flux = f * (0.5 * (la[k] + ln[k])) * (d + density[k] * gravity_step)
                net[k, x, at, :] = sums[k] + (flux - lane_prev(flux))
            cz[x, at, :] = f * (0.5 * (lt + (ln[0] + ln[1] + ln[2])))
        e4[3, one, :] = cy[x, pl.ds(CY, 1), :]
        return tuple(tuple(v) for v in below[:3])

    first = tuple(tuple(v[8 * c : 8 * c + 8] for c in range(4)) for v in below[:3])
    half = loop(0, CX // 2, fluxes, first, 4)
    for k in range(1, NGX):
        source = place_y * NGX + lax.rem(place_x + NGX - k, NGX)
        there = wells.at[:, pl.ds(source, 1), :]
        remote(there, there, send_x.at[k], recv_x.at[k], lax.rem(place_x + k, NGX), place_y).wait_recv()
    block = wells.at[:, pl.ds(place_y * NGX, NGX), :]
    for k in range(1, NGY):
        copy = remote(block, block, send_y.at[k], recv_y.at[k], place_x, lax.rem(place_y + k, NGY))
        copy.start()
        sends.append(copy)
    loop(CX // 2, CX, fluxes, half, 4)
    for src, dst in ((net, net_o), (cx, cx_o), (cy, cy_o), (cz, cz_o)):
        give(src, dst)

    zero = jnp.zeros((8, NZ), f32)

    def crossings(x, sums):
        sums = list(sums)
        for c in range(4):
            at = pl.ds(8 * c, 8)
            up = pl.ds(8 * c + 1, 8)
            a = agg[x, at, :]
            for b, e, ok in (
                (agg[x + 1, at, :], cx[x + 1, at, :], x < CX - 1),
                (agg[x, up, :], cy[x, up, :], (row_8 < 7) if c == 3 else None),
            ):
                code = jnp.minimum(a, b) * GROUPS + jnp.maximum(a, b)
                if ok is not None:
                    code = jnp.where(ok, code, -1)
                for n, (g, h) in enumerate(PAIRS):
                    sums[n] = sums[n] + jnp.where(code == g * GROUPS + h, e, 0.0)
            cross = jnp.where(a != lane_next(a), cz[x, at, :], 0.0)
            for n, (g, h) in enumerate(PAIRS):
                if h == g + 1:
                    sums[n] = sums[n] + jnp.where(a == g, cross, 0.0)
        return tuple(sums)

    acc[...] = jnp.zeros_like(acc)
    sums = loop(0, CX, crossings, (zero,) * len(PAIRS), 2)
    for n, (g, h) in enumerate(PAIRS):
        v = line(sums[n])[0]
        acc[h * GROUPS + g, :] = v
        acc[g * GROUPS + h, :] = v

    e4[0] = cx[0]
    e4[1] = cx[CX]
    own4[0] = agg[0, pl.ds(0, CY), :]
    own4[1] = agg[CX - 1, pl.ds(0, CY), :]
    nb4[0] = xlo_i[1]
    nb4[1] = xhi_i[1]
    nb4[2] = ylo_i[1]
    nb4[3] = yhi_i[1]
    give(nb4, nb_o)

    def side(d, _):
        e, a, b = e4[d], own4[d], nb4[d]
        for h in range(GROUPS):
            w = jnp.where(b == h, e, 0.0)
            rows = [line(jnp.where(a == g, w, 0.0)) for g in range(GROUPS)]
            start = pl.multiple_of(((d + 1) * GROUPS + h) * GROUPS, 8)
            acc[pl.ds(start, GROUPS), :] = jnp.concatenate(rows, axis=0)
        return 0

    lax.fori_loop(0, 4, side, 0)
    for n in range(3):
        sums_o[n] = jnp.sum(acc[pl.ds(NZ * n, NZ), :].T, axis=0, keepdims=True)
    for k in range(1, NGY):
        source = lax.rem(place_y + NGY - k, NGY)
        there = wells.at[:, pl.ds(source * NGX, NGX), :]
        remote(there, there, send_y.at[k], recv_y.at[k], place_x, lax.rem(place_y + k, NGY)).wait_recv()
    for copy in sends + faces:
        copy.wait_send()
    for copy in outs:
        copy.wait()


BLK = (CX, CY, NZ)


def exchange(p, ws, gs, act, tx, ty, tz, agg, cells, windex, hole):
    sds = jax.ShapeDtypeStruct
    dma = pltpu.SemaphoreType.DMA
    v = pltpu.VMEM
    face = lambda n, t: v((n, 32, NZ), t)
    return pl.pallas_call(
        exchange_kernel,
        out_shape=[
            sds((3,) + BLK, f32), sds((CX + 1, CY, NZ), f32), sds((CX, CY + 8, NZ), f32), sds(BLK, f32), sds(BLK, f32),
            sds((3, 1, NZ), f32), sds((4, 32, NZ), i32), sds((2, NDEV, NZ), f32),
        ],
        in_specs=[ANY] * 8 + [VMEM, VMEM, SMEM],
        out_specs=[ANY] * 5 + [VMEM, ANY, VMEM],
        scratch_shapes=[
            v((CX + 1, CY + 8, NZ), f32), v(BLK, f32), v(BLK, f32), v(BLK, i32),
            v(BLK, f32), v(BLK, f32), v(BLK, f32), v((CX + 1, CY + 8, NZ), i32),
            face(4, f32), face(2, i32), face(3, f32), face(2, i32), face(4, f32), face(2, i32), face(3, f32), face(2, i32),
            v((3, CX + 1, CY + 8, NZ), f32), v((CX + 1, CY + 8, NZ), f32), v(BLK, f32), v((3,) + BLK, f32),
            v((3, CX, CY + 8, NZ), f32), v((CX + 1, CY, NZ), f32), v((CX, CY + 8, NZ), f32), v(BLK, f32),
            face(10, f32), v((ROWS, NZ), f32), face(4, f32), face(4, i32), face(4, i32),
            dma((8,)), dma((8,)), dma((22,)), dma((22,)), dma((NGX,)), dma((NGX,)), dma((NGY,)), dma((NGY,)),
        ],
        compiler_params=pltpu.CompilerParams(collective_id=0, has_side_effects=True, vmem_limit_bytes=BIG),
        name="exchange",
    )(p, ws, gs, act, tx, ty, tz, agg, cells, windex, hole)


def local_kernel(
    p_h, ws_h, gs_h, old_h, pv_h, act_h, agg_h, mob_h, net_h, cx_h, cy_h, cz_h, nb_h, wells, sums,
    res_o, t_o, dinv_o, sums_o, faces_o, parts_o,
    p, ws, gs, act, agg, old, pv, net, cx, cy, cz, nb4,
    mob, w0, w1, trows, loc, loc_s, s, rem, leak, dinv, res, t, acc, s4,
    sem, out_sem, one_sem,
):
    place_x, place_y = lax.axis_index("gx"), lax.axis_index("gy")
    copies = []

    def fetch(src, dst):
        copy = pltpu.make_async_copy(src, dst, sem.at[len(copies)])
        copy.start()
        copies.append(copy)

    fetch(mob_h, mob)
    fetch(p_h, p)
    early = len(copies)
    for src, dst in (
        (ws_h, ws), (gs_h, gs), (act_h, act), (pv_h, pv), (old_h, old), (net_h, net), (cx_h, cx), (cy_h, cy), (cz_h, cz),
        (agg_h, agg), (nb_h, nb4),
    ):
        fetch(src, dst)

    lane = iota((NDEV, NZ), 1)
    table = wells[0]
    cell = table.astype(i32)
    cell_x, cell_y, layer = cell >> 16, (cell >> 7) & 511, cell & 127
    slot = lane & 31
    here = (slot < PERF) & (cell >= 0) & ((cell_x >> 5) == place_x) & ((cell_y >> 5) == place_y)
    local = ((((cell_x & 31) << 5) + (cell_y & 31)) << 7) + layer
    local = jnp.where(here, local, -1)
    flag = jnp.where(here, 1.0, 0.0).astype(jnp.bfloat16)
    at_in, at_out = iota((NZ, NZ), 0), iota((NZ, NZ), 1)
    pick = ((at_in // 32 == at_out // 32) & (at_out % 32 == 16)) | (at_out == 17)
    counts = jnp.dot(flag, jnp.where(pick, 1.0, 0.0).astype(jnp.bfloat16), preferred_element_type=f32).astype(i32)
    first_layer = pltpu.roll(layer, 18, 1)
    loc[...] = jnp.where(slot < PERF, local, jnp.where(slot == 18, first_layer, counts))
    to_scalar = pltpu.make_async_copy(loc, loc_s, one_sem)
    to_scalar.start()

    w0[...] = jnp.zeros_like(w0)
    w1[...] = jnp.zeros_like(w1)
    trows[...] = jnp.zeros_like(trows)
    for copy in copies[:early]:
        copy.wait()
    to_scalar.wait()

    row_lane = iota((1, NZ), 1)

    def one_row(r, _):
        @pl.when(loc_s[r, 17] > 0)
        def _():
            for j in range(4):

                @pl.when(loc_s[r, 32 * j + 16] > 0)
                def _():
                    shift = loc_s[r, 32 * j + 18] - (32 * j + PERF) + 2 * NZ
                    shift = lax.rem(shift, NZ)
                    index_z = pltpu.roll(wells[0, pl.ds(r, 1), :], shift, 1)
                    hole_z = pltpu.roll(wells[1, pl.ds(r, 1), :], shift, 1)
                    drive_z = index_z * hole_z
                    mob_z = jnp.zeros((1, NZ), f32)
                    press_z = jnp.zeros((1, NZ), f32)
                    for k in range(PERF):
                        at = loc_s[r, 32 * j + k]
                        z = (at & 127) | (at >> 31)
                        q = jnp.maximum(at, 0) >> 7
                        qx, qy = q >> 5, q & 31
                        hit = row_lane == z
                        w0[qx, pl.ds(qy, 1), :] += jnp.where(hit, index_z, 0.0)
                        w1[qx, pl.ds(qy, 1), :] += jnp.where(hit, drive_z, 0.0)
                        mob_z = jnp.where(hit, mob[qx, pl.ds(qy, 1), :], mob_z)
                        press_z = jnp.where(hit, p[qx, pl.ds(qy, 1), :], press_z)
                    well = ((r & (NGX - 1)) * NGY + (r >> 3)) * 4 + j
                    trows[pl.ds(well, 1), :] = index_z * mob_z * (hole_z - press_z)

        return 0

    loop(0, NDEV, one_row, 0, 4)
    total = lax.dot_general(
        jnp.ones((8, NZ), f32), trows[...], (((1,), (1,)), ((), ())), precision=precise, preferred_element_type=f32
    )
    sub = iota((8, NZ), 0)
    parts = jnp.zeros((8, NZ), f32)
    for k in range(NGX):
        piece = total[:, NZ * (k // 2) : NZ * (k // 2) + NZ]
        if k % 2:
            piece = pltpu.roll(piece, 64, 1)
        parts = jnp.where(sub == k, piece, parts)
    parts_o[...] = parts

    for copy in copies[early:]:
        copy.wait()

    def residuals(x, _):
        for c in range(4):
            at = pl.ds(8 * c, 8)
            z = cz[x, at, :]
            diag = (cx[x + 1, at, :] + cx[x, at, :]) + (cy[x, pl.ds(8 * c + 1, 8), :] + cy[x, at, :]) + (z + lane_prev(z))
            pp, m = p[x, at, :], act[x, at, :].astype(f32)
            sw, sg = ws[x, at, :], gs[x, at, :]
            so = 1.0 - sw - sg
            vol = pv[x, at, :]
            wa, wb = w0[x, at, :], w1[x, at, :]
            pull = m * (wb - pp * wa)
            rhs = None
            for k, sat in enumerate((sw, so, sg)):
                held = (1.0 + compress[k] * (pp - 1.0)) * sat
                r = m * (vol * (held - old[k, x, at, :]) + net[k, x, at, :]) - pull * (held * sat * (1.0 / viscosity[k]))
                res[k, x, at, :] = r
                rhs = r if rhs is None else rhs + r
            rhs = -rhs
            store = vol * (compress[0] * sw + compress[1] * so + compress[2] * sg)
            lk = m * store + wa * mob[x, at, :] + dead_leak * (1.0 - m)
            leak[x, at, :] = lk
            diag = diag + lk
            di = relax / diag
            dinv[x, at, :] = di
            sm = rhs * di
            s[x + 1, pl.ds(8 * c + 1, 8), :] = sm
            rem[x, at, :] = rhs - diag * sm
        one = pl.ds(x, 1)
        s4[2, one, :] = s[x + 1, pl.ds(1, 1), :]
        s4[3, one, :] = s[x + 1, pl.ds(CY, 1), :]
        s[x + 1, pl.ds(0, 1), :] = jnp.zeros((1, NZ), f32)
        s[x + 1, pl.ds(CY + 1, 1), :] = jnp.zeros((1, NZ), f32)
        return 0

    loop(0, CX, residuals, 0, 4)
    s4[0] = s[1, pl.ds(1, CY), :]
    s4[1] = s[CX, pl.ds(1, CY), :]
    s[0] = jnp.zeros_like(s[0])
    s[CX + 1] = jnp.zeros_like(s[0])
    outs = []

    def give(src, dst):
        copy = pltpu.make_async_copy(src, dst, out_sem.at[len(outs)])
        copy.start()
        outs.append(copy)

    give(res, res_o)
    give(dinv, dinv_o)
    give(s4, faces_o)

    zero = jnp.zeros((8, NZ), f32)

    def remainders(x, carry):
        lk_sum, re_sum = [list(v) for v in carry]
        for c in range(4):
            at = pl.ds(8 * c, 8)
            up = pl.ds(8 * c + 1, 8)
            here = s[x + 1, up, :]
            z = cz[x, at, :]
            near = cx[x + 1, at, :] * s[x + 2, up, :] + cx[x, at, :] * s[x, up, :]
            near = near + (cy[x, up, :] * s[x + 1, pl.ds(8 * c + 2, 8), :] + cy[x, at, :] * s[x + 1, at, :])
            near = near + (z * lane_next(here) + lane_prev(z * here))
            re = rem[x, at, :] + near
            t[x, at, :] = here + dinv[x, at, :] * re
            lk = leak[x, at, :]
            a = agg[x, at, :]
            for g in range(GROUPS):
                hit = a == g
                re_sum[g] = re_sum[g] + jnp.where(hit, re, 0.0)
                lk_sum[g] = lk_sum[g] + jnp.where(hit, lk, 0.0)
        return tuple(lk_sum), tuple(re_sum)

    lk_sum, re_sum = loop(0, CX, remainders, ((zero,) * GROUPS, (zero,) * GROUPS), 4)
    give(t, t_o)
    rows = [line(v) for v in re_sum]
    acc[...] = jnp.zeros_like(acc)
    for n in range(2):
        coef = (cx[0], cx[CX])[n]
        es = coef * s4[n]
        rows += [line(jnp.where(nb4[n] == g, es, 0.0)) for g in range(GROUPS)]
    e4 = trows
    for x in range(CX):
        e4[pl.ds(x, 1), :] = cy[x, pl.ds(0, 1), :]
        e4[pl.ds(CX + x, 1), :] = cy[x, pl.ds(CY, 1), :]
    for n in range(2):
        es = e4[pl.ds(CX * n, CX), :] * s4[2 + n]
        rows += [line(jnp.where(nb4[2 + n] == g, es, 0.0)) for g in range(GROUPS)]
    rows += [line(v) for v in lk_sum]
    first = RHS_AT - 2 * NZ
    for n in range(6):
        acc[pl.ds(first + 8 * n, 8), :] = jnp.concatenate(rows[8 * n : 8 * n + 8], axis=0)
    sums_o[0] = sums[0]
    sums_o[1] = sums[1]
    sums_o[2] = sums[2] + jnp.sum(acc[...].T, axis=0, keepdims=True)
    for copy in outs:
        copy.wait()


def local(p, ws, gs, old, pv, act, agg, mob, net, cx, cy, cz, nb, wells, sums):
    v = pltpu.VMEM
    sds = jax.ShapeDtypeStruct
    dma = pltpu.SemaphoreType.DMA
    return pl.pallas_call(
        local_kernel,
        out_shape=[
            sds((3,) + BLK, f32), sds(BLK, f32), sds(BLK, f32), sds((3, 1, NZ), f32), sds((4, 32, NZ), f32), sds((8, NZ), f32)
        ],
        in_specs=[ANY] * 13 + [VMEM, VMEM],
        out_specs=[ANY] * 3 + [VMEM, ANY, VMEM],
        scratch_shapes=[
            v(BLK, f32), v(BLK, f32), v(BLK, f32), v(BLK, i32), v(BLK, i32), v((3,) + BLK, f32), v(BLK, f32),
            v((3,) + BLK, f32), v((CX + 1, CY, NZ), f32), v((CX, CY + 8, NZ), f32), v(BLK, f32), v((4, 32, NZ), i32),
            v(BLK, f32), v(BLK, f32), v(BLK, f32), v((4 * NDEV, NZ), f32), v((NDEV, NZ), i32), pltpu.SMEM((NDEV, NZ), i32),
            v((CX + 2, CY + 8, NZ), f32), v(BLK, f32), v(BLK, f32), v(BLK, f32), v((3,) + BLK, f32), v(BLK, f32),
            v((NZ, NZ), f32), v((4, 32, NZ), f32),
            dma((16,)), dma((8,)), dma,
        ],
        compiler_params=pltpu.CompilerParams(vmem_limit_bytes=BIG),
        name="local",
    )(p, ws, gs, old, pv, act, agg, mob, net, cx, cy, cz, nb, wells, sums)


def coarse_kernel(
    sums, parts, faces, t_h, dinv_h, cx_h, cy_h, cz_h, agg_h, nb4,
    update_o, well_o,
    gather, mat, slots, send_rows, rows_x, rows_y, tall, dinv, cx, cy, cz, agg, far, pc,
    sem, send_x, recv_x, send_y, recv_y, psend_x, precv_x, psend_y, precv_y, fsend, frecv,
):
    place_x, place_y = lax.axis_index("gx"), lax.axis_index("gy")
    me = place_y * NGX + place_x
    barrier = pltpu.get_barrier_semaphore()
    greet(barrier)
    loads = []
    body = (slice(None), pl.ds(0, CY), slice(None))
    for src, dst in ((t_h, tall), (dinv_h, dinv), (cx_h, cx), (cy_h, cy), (cz_h, cz), (agg_h, agg)):
        copy = pltpu.make_async_copy(src, dst, sem.at[len(loads)])
        copy.start()
        loads.append(copy)
    for n in range(3):
        gather[n, pl.ds(me, 1), :] = sums[n]
    rows_x[pl.ds(place_x, 1), :] = parts[pl.ds(place_x, 1), :]
    pl.semaphore_wait(barrier, NGX - 1 + NGY - 1)

    sends = []
    own = gather.at[:, pl.ds(me, 1), :]
    for k in range(1, NGX):
        peer = lax.rem(place_x + k, NGX)
        sends.append(remote(own, own, send_x.at[k], recv_x.at[k], peer, place_y))
    for k in range(1, NGX):
        peer = lax.rem(place_x + k, NGX)
        sends.append(
            remote(parts.at[pl.ds(peer, 1), :], rows_x.at[pl.ds(place_x, 1), :], psend_x.at[k], precv_x.at[k], peer, place_y)
        )
    halo = [
        remote(faces.at[1], far.at[0], fsend.at[0], frecv.at[0], lax.rem(place_x + 1, NGX), place_y),
        remote(faces.at[0], far.at[1], fsend.at[1], frecv.at[1], lax.rem(place_x + NGX - 1, NGX), place_y),
        remote(faces.at[3], far.at[2], fsend.at[2], frecv.at[2], place_x, lax.rem(place_y + 1, NGY)),
        remote(faces.at[2], far.at[3], fsend.at[3], frecv.at[3], place_x, lax.rem(place_y + NGY - 1, NGY)),
    ]
    for copy in sends + halo:
        copy.start()
    for k in range(1, NGX):
        source = place_y * NGX + lax.rem(place_x + NGX - k, NGX)
        there = gather.at[:, pl.ds(source, 1), :]
        remote(there, there, send_x.at[k], recv_x.at[k], place_x, place_y).wait_recv()
    block = gather.at[:, pl.ds(place_y * NGX, NGX), :]
    for k in range(1, NGY):
        copy = remote(block, block, send_y.at[k], recv_y.at[k], place_x, lax.rem(place_y + k, NGY))
        copy.start()
        sends.append(copy)
    for k in range(1, NGX):
        source = lax.rem(place_x + NGX - k, NGX)
        there = rows_x.at[pl.ds(source, 1), :]
        remote(there, there, psend_x.at[k], precv_x.at[k], place_x, place_y).wait_recv()
    line = jnp.sum(rows_x[...], axis=0, keepdims=True)
    for k in range(NGY):
        send_rows[k : k + 1, :] = line if k == 0 else pltpu.roll(line, NZ - 4 * k, 1)
    rows_y[pl.ds(place_y, 1), :] = send_rows[pl.ds(place_y, 1), :]
    for k in range(1, NGY):
        peer = lax.rem(place_y + k, NGY)
        copy = remote(
            send_rows.at[pl.ds(peer, 1), :], rows_y.at[pl.ds(place_y, 1), :], psend_y.at[k], precv_y.at[k], place_x, peer
        )
        copy.start()
        sends.append(copy)
    for k in range(1, NGY):
        source = lax.rem(place_y + NGY - k, NGY)
        there = gather.at[:, pl.ds(source * NGX, NGX), :]
        remote(there, there, send_y.at[k], recv_y.at[k], place_x, place_y).wait_recv()

    for n in range(3):
        mat[pl.ds(NZ * n, NZ), :] = gather[n].T
    sub = iota((8, NZ), 0)

    def rows(n):
        return mat[pl.ds(8 * n, 8), :]

    moves = (0, 1, NZ - 1, NGX, NZ - NGX)
    total = jnp.zeros((8, NZ), f32)
    for n in range(5 * GROUPS):
        total = total + rows(n)
    total = total + rows(LEAK_AT // 8)
    for h in range(GROUPS):
        block = rows(h)
        slots[pl.ds(8 * h, 8), :] = jnp.where(sub == h, total, -block)
    for d in range(1, 5):
        for h in range(GROUPS):
            v = -rows(d * GROUPS + h)
            slots[pl.ds((d * GROUPS + h) * 8, 8), :] = pltpu.roll(v, (NZ - moves[d]) % NZ, 1)
    rhs = rows(RHS_AT // 8)
    for d in range(1, 5):
        away = (0, 2, 1, 4, 3)[d]
        rhs = rhs + pltpu.roll(rows(OUT_AT // 8 + away - 1), moves[d], 1)

    def dot(a, b):
        return jnp.sum(jnp.sum(a * b, axis=0, keepdims=True), axis=1, keepdims=True)

    def one_step(_, carry):
        x, r, q, rr = carry
        sums5 = [None] * 5
        for h in range(GROUPS):
            spread = jnp.broadcast_to(q[h : h + 1, :], (8, NZ))
            for d in range(5):
                v = slots[pl.ds((d * GROUPS + h) * 8, 8), :] * spread
                sums5[d] = v if sums5[d] is None else sums5[d] + v
        image = sums5[0]
        for d in range(1, 5):
            image = image + pltpu.roll(sums5[d], moves[d], 1)
        alpha = rr / dot(q, image)
        x = x + alpha * q
        r = r - alpha * image
        new = dot(r, r)
        q = r + (new / rr) * q
        return x, r, q, new

    coarse = loop(0, CITERS, one_step, (jnp.zeros((8, NZ), f32), rhs, rhs, dot(rhs, rhs)), 4)[0]
    mine = iota((8, NZ), 1) == me
    values = []
    for d in range(5):
        v = coarse if d == 0 else pltpu.roll(coarse, moves[d], 1)
        values.append(jnp.sum(jnp.where(mine, v, 0.0), axis=1, keepdims=True))

    def look_up(ids, d):
        v = jnp.broadcast_to(values[d][0:1, :], ids.shape)
        for g in range(1, GROUPS):
            v = jnp.where(ids == g, values[d][g : g + 1, :], v)
        return v

    for copy in halo:
        copy.wait_recv()
    for copy in loads:
        copy.wait()
    pc[0, pl.ds(8, CY), :] = far[0] + look_up(nb4[0], 1)
    pc[CX + 1, pl.ds(8, CY), :] = far[1] + look_up(nb4[1], 2)
    far[2] = far[2] + look_up(nb4[2], 3)
    far[3] = far[3] + look_up(nb4[3], 4)

    def fill(x, _):
        pc[x + 1, pl.ds(8, CY), :] = look_up(agg[x], 0)
        pc[x + 1, pl.ds(7, 1), :] = far[2, pl.ds(x, 1), :]
        pc[x + 1, pl.ds(CY + 8, 1), :] = far[3, pl.ds(x, 1), :]
        return 0

    loop(0, CX, fill, 0, 8)

    def finish(x, _):
        for c in range(4):
            at = pl.ds(8 * c, 8)
            mid = pl.ds(8 * c + 8, 8)
            here = pc[x + 1, mid, :]
            z = cz[x, at, :]
            near = cx[x + 1, at, :] * pc[x + 2, mid, :] + cx[x, at, :] * pc[x, mid, :]
            near = near + (
                cy[x, pl.ds(8 * c + 1, 8), :] * pc[x + 1, pl.ds(8 * c + 9, 8), :]
                + cy[x, at, :] * pc[x + 1, pl.ds(8 * c + 7, 8), :]
            )
            near = near + (z * lane_next(here) + lane_prev(z * here))
            update_o[x, at, :] = tall[x, at, :] + (1.0 - relax) * here + dinv[x, at, :] * near
        return 0

    loop(0, CX, finish, 0, 8)
    for k in range(1, NGY):
        source = lax.rem(place_y + NGY - k, NGY)
        there = rows_y.at[pl.ds(source, 1), :]
        remote(there, there, psend_y.at[k], precv_y.at[k], place_x, place_y).wait_recv()
    well_o[...] = jnp.sum(rows_y[...], axis=0, keepdims=True)
    for copy in sends + halo:
        copy.wait_send()


def coarse_part(sums, parts, faces, t, dinv, cx, cy, cz, agg, nb4):
    v = pltpu.VMEM
    sds = jax.ShapeDtypeStruct
    dma = pltpu.SemaphoreType.DMA
    return pl.pallas_call(
        coarse_kernel,
        out_shape=[sds(BLK, f32), sds((1, NZ), f32)],
        in_specs=[VMEM, VMEM, ANY] + [ANY] * 6 + [VMEM],
        out_specs=[VMEM, VMEM],
        scratch_shapes=[
            v((3, NDEV, NZ), f32), v((ROWS, NZ), f32), v((5 * 64, NZ), f32), v((NGY, NZ), f32), v((NGX, NZ), f32), v((NGY, NZ), f32),
            v(BLK, f32), v(BLK, f32), v((CX + 1, CY, NZ), f32), v((CX, CY + 8, NZ), f32), v(BLK, f32), v(BLK, i32),
            v((4, 32, NZ), f32), v((CX + 2, CY + 16, NZ), f32),
            dma((8,)), dma((NGX,)), dma((NGX,)), dma((NGY,)), dma((NGY,)),
            dma((NGX,)), dma((NGX,)), dma((NGY,)), dma((NGY,)), dma((4,)), dma((4,)),
        ],
        compiler_params=pltpu.CompilerParams(
            collective_id=1, has_side_effects=True, vmem_limit_bytes=BIG
        ),
        name="coarse",
    )(sums, parts, faces, t, dinv, cx, cy, cz, agg, nb4)


def per_device(
    pressure, water_sat, gas_sat, old_content, pore_volume, trans_x, trans_y, trans_z, active, aggregate,
    well_cells, well_index, bottom_hole, well_target,
):
    net, cx, cy, cz, mob, sums, nb, wells = exchange(
        pressure, water_sat, gas_sat, active, trans_x, trans_y, trans_z, aggregate, well_cells, well_index, bottom_hole
    )
    residual, t, dinv, sums, faces, parts = local(
        pressure, water_sat, gas_sat, old_content, pore_volume, active, aggregate, mob, net, cx, cy, cz, nb, wells, sums
    )
    update, well = coarse_part(sums, parts, faces, t, dinv, cx, cy, cz, aggregate, nb)
    return residual, update, well[0, :4] - well_target


def solution(mesh):
    cells = P("gx", "gy", None)
    three = P(None, "gx", "gy", None)
    well, one = P(("gx", "gy"), None), P(("gx", "gy"))
    return jax.shard_map(
        per_device,
        mesh=mesh,
        in_specs=(cells, cells, cells, three) + (cells,) * 6 + (well, well, one, one),
        out_specs=(three, cells, one),
        check_vma=False,
    )
```

time: 69.1 us -> 59.8 us (0.87)
  Pallas kernels: 65.1 us -> 55.9 us
    pallas_call x3, Pallas kernels: 65.1 us -> 55.9 us  [the longest x1 23.6 us: exchange(): pl.pallas_call(exchange_kernel, out_shape=[sds((3,) + BLK, f32), sds((CX...]
where the time goes in v2:
time: 59.8 us; the launch traced here: 59.5 us
  Pallas kernels  55.9 us (93%)
  local copies, waits for them, and re-layouts  1.87 us (3%)
  other arithmetic  1.09 us (2%)
  between operations  0.67 us (1%)
    pallas_call x1, Pallas kernels, exchange(): pl.pallas_call(exchange_kernel, out_shape=[sds((3,) + BLK, f32), sds((CX...  23.6 us
    pallas_call x1, Pallas kernels, coarse_part(): pl.pallas_call(coarse_kernel, out_shape=[sds(BLK, f32), sds((1, NZ), f32)...  22.7 us
    pallas_call x1, Pallas kernels, local(): pl.pallas_call(local_kernel, out_shape=[sds((3,) + BLK, f32), sds(BLK, f3...  9.67 us
    unnamed x3, local copies, waits for them, and re-layouts  1.87 us

profile of v2, /device:TPU:1, one launch (start us, length us, event | category | flops | bytes accessed | tf_op | source)
XLA Modules:
  0.0 59.5 jit_solution(9960896676098847911)
XLA Ops:
  0.6 23.6 %exchange.1 = (f32[3,32,32,128]{3,2,1,0:T(8,128)}, f32[33,32,128]{2,1,0:T(8,128)}, f32[32,40,128]{2,1,0:T(8,128)}, f32[32,32,128]{2,1,0:T(8,128)}, f32[32,32,128...) custom-call(f32[32,32,128]{2,1,0:T(8,128)} %p_h.3, f32[32,32,128]{2,1,0:T(8,128)} %ws_h.3, ...), custom_call_target="tpu_custom_call" | custom-call | tf_op jit(solution)/shard_map/exchange/pallas_call | solution.py:342
  24.2 9.7 %local.1 = (f32[3,32,32,128]{3,2,1,0:T(8,128)}, f32[32,32,128]{2,1,0:T(8,128)}, f32[32,32,128]{2,1,0:T(8,128)}, f32[3,1,128]{2,1,0:T(1,128)}, f32[4,32,128]{2,1,0:T(8,128)}, /*index=5*/f32[8,128]{1,0:T(8,128)}) custom-call(f32[32,32,128]{2,1,0:T(8,128)} %p_h.3, f32[32,32,128]{2,1,0:T(8,128)} %ws_h.3, f32[32,32,128]{2,1,0:T(8,128)} %gs_h.3, ...), custom_call_target="tpu_custom_call" | custom-call | tf_op jit(solution)/shard_map/local/pallas_call | solution.py:561
  33.9 0.0 copy-start
  33.9 22.7 %coarse.1 = (f32[32,32,128]{2,1,0:T(8,128)}, f32[1,128]{1,0:T(1,128)}) custom-call(f32[3,1,128]{2,1,0:T(1,128)} %get-tuple-element.28.sums, f32[8,128]{1,0:T(8,128)} %get-tuple-element.29.parts, f32[4,32,128]{2,1,0:T(8,128)} %get-tuple-element.30.faces, f32[32,32,128]{2,1,0:T(8,128)} %get-tuple-element.31.t_h, f32[32,32,128]{2,1,0:T(8,128)} %get-tuple-element.32.dinv_h, ...), custom_call_target="tpu_custom_call" | custom-call | tf_op jit(solution)/shard_map/coarse/pallas_call | solution.py:753
  56.6 0.0 copy-done
  56.6 1.1 %bitcast_subtract_fusion = f32[4]{0:T(128)} fusion(f32[4]{0:T(128)S(1)} %copy-done, f32[1,128]{1,0:T(1,128)} %get-tuple-element.34), kind=kLoop, calls=%fused_computation | loop fusion | flops 4 | bytes 48 | tf_op jit(solution)/shard_map/sub | solution.py:783
  57.7 1.9 %copy.18 = f32[32,32,128]{2,1,0:T(8,128)} copy(f32[32,32,128]{2,1,0:T(8,128)} %get-tuple-element.39) | data formatting | bytes 1048576
Async XLA Ops:
  33.9 22.7 %copy-start = (f32[4]{0:T(128)S(1)}, f32[4]{0:T(128)}, u32[]{:S(2)}) copy-start(f32[4]{0:T(128)} %param.27) | copy-start | bytes 52

commit v3 on v2

--- a/solution.py
+++ b/solution.py
@@ -85,7 +85,7 @@
     p_h, ws_h, gs_h, act_h, tx_h, ty_h, tz_h, agg_h, cells, windex, hole,
     net_o, cx_o, cy_o, cz_o, mob_o, sums_o, nb_o, wells,
     p, ws, gs, act, tx, ty, tz, agg, xlo_f, xlo_i, xhi_f, xhi_i, ylo_f, ylo_i, yhi_f, yhi_i,
-    lam, live, mob, net, fy, cx, cy, cz, yh, acc, e4, own4, nb4,
+    lam, live, mob, net, fy, cx, cy, cz, rim, acc, e4, own4, nb4,
     load_sem, out_sem, face_send, face_recv, send_x, recv_x, send_y, recv_y,
 ):
     place_x, place_y = lax.axis_index("gx"), lax.axis_index("gy")
@@ -154,8 +154,27 @@
         m = act[x].astype(f32)
         live[x, pl.ds(0, CY), :] = m
         mob[x] = m * (parts[0] + parts[1] + parts[2])
+        none = jnp.zeros((1, NZ), f32)
+        for k in range(3):
+            lam[k, x, pl.ds(CY, 1), :] = none
+            fy[k, x, pl.ds(0, 1), :] = none
+        p[x, pl.ds(CY, 1), :] = none
+        live[x, pl.ds(CY, 1), :] = none
+        agg[x, pl.ds(CY, 1), :] = jnp.zeros((1, NZ), i32)
+        cy[x, pl.ds(0, 1), :] = none
+        one = pl.ds(x, 1)
+        for side, y in ((0, 0), (1, CY - 1)):
+            for k in range(3):
+                rim[side, k, one, :] = parts[k][y : y + 1]
+            rim[side, 3, one, :] = p[x, pl.ds(y, 1), :]
+            rim[side, 4, one, :] = m[y : y + 1]
         return 0
 
+    for k in range(3):
+        lam[k, CX] = jnp.zeros((CY + 8, NZ), f32)
+    p[CX] = jnp.zeros((CY + 8, NZ), f32)
+    live[CX] = jnp.zeros((CY + 8, NZ), f32)
+    agg[CX] = jnp.zeros((CY + 8, NZ), i32)
     loop(0, CX, mobilities, 0, 8)
     outs = []
 
@@ -167,58 +186,11 @@
     give(mob, mob_o)
     for copy in loads[4:]:
         copy.wait()
-    for copy in faces:
-        copy.wait_recv()
-
-    end_x = jnp.where(place_x == NGX - 1, 0.0, 1.0)
-    end_y = jnp.where(place_y == NGY - 1, 0.0, 1.0)
-    dead_x = jnp.where(place_x == 0, 0.0, 1.0)
-    dead_y = jnp.where(place_y == 0, 0.0, 1.0)
-    high = mobility_of(xhi_f[0], xhi_f[1], xhi_f[2])
-    for k in range(3):
-        lam[k, CX, pl.ds(0, CY), :] = high[k]
-    p[CX, pl.ds(0, CY), :] = xhi_f[0]
-    live[CX, pl.ds(0, CY), :] = xhi_i[0].astype(f32) * end_x
-    agg[CX, pl.ds(0, CY), :] = xhi_i[1]
-    low = mobility_of(xlo_f[0], xlo_f[1], xlo_f[2])
-    face_trans = xlo_f[3] * (xlo_i[0].astype(f32) * dead_x) * live[0, pl.ds(0, CY), :]
-    drop = xlo_f[0] - p[0, pl.ds(0, CY), :]
-    high = [lam[k, 0, pl.ds(0, CY), :] for k in range(3)]
-    below = [face_trans * (0.5 * (low[k] + high[k])) * drop for k in range(3)]
-    below.append(face_trans * (0.5 * ((low[0] + low[1] + low[2]) + (high[0] + high[1] + high[2]))))
-    cx[0] = below[3]
-    low = mobility_of(ylo_f[0], ylo_f[1], ylo_f[2])
-    for k in range(3):
-        yh[k] = low[k]
-    yh[3] = ylo_f[0]
-    yh[4] = ylo_f[3] * (ylo_i[0].astype(f32) * dead_y)
-    high = mobility_of(yhi_f[0], yhi_f[1], yhi_f[2])
-    for k in range(3):
-        yh[5 + k] = high[k]
-    yh[8] = yhi_f[0]
-    yh[9] = yhi_i[0].astype(f32) * end_y
     layer_8 = iota((8, NZ), 1)
     row_8 = iota((8, NZ), 0)
 
     def fluxes(x, carry):
         below = [list(v) for v in carry]
-        one = pl.ds(x, 1)
-        for k in range(3):
-            lam[k, x, pl.ds(CY, 1), :] = yh[5 + k, one, :]
-        p[x, pl.ds(CY, 1), :] = yh[8, one, :]
-        live[x, pl.ds(CY, 1), :] = yh[9, one, :]
-        agg[x, pl.ds(CY, 1), :] = yhi_i[1, one, :]
-        own4[2, one, :] = agg[x, pl.ds(0, 1), :]
-        own4[3, one, :] = agg[x, pl.ds(CY - 1, 1), :]
-        face0 = yh[4, one, :] * live[x, pl.ds(0, 1), :]
-        drop0 = yh[3, one, :] - p[x, pl.ds(0, 1), :]
-        up0 = [lam[k, x, pl.ds(0, 1), :] for k in range(3)]
-        dn0 = [yh[k, one, :] for k in range(3)]
-        for k in range(3):
-            fy[k, x, pl.ds(0, 1), :] = face0 * (0.5 * (dn0[k] + up0[k])) * drop0
-        cy0 = face0 * (0.5 * ((dn0[0] + dn0[1] + dn0[2]) + (up0[0] + up0[1] + up0[2])))
-        cy[x, pl.ds(0, 1), :] = cy0
-        e4[2, one, :] = cy0
         for c in range(4):
             at = pl.ds(8 * c, 8)
             up = pl.ds(8 * c + 1, 8)
@@ -251,10 +223,10 @@
                 flux = f * (0.5 * (la[k] + ln[k])) * (d + density[k] * gravity_step)
                 net[k, x, at, :] = sums[k] + (flux - lane_prev(flux))
             cz[x, at, :] = f * (0.5 * (lt + (ln[0] + ln[1] + ln[2])))
-        e4[3, one, :] = cy[x, pl.ds(CY, 1), :]
         return tuple(tuple(v) for v in below[:3])
 
-    first = tuple(tuple(v[8 * c : 8 * c + 8] for c in range(4)) for v in below[:3])
+    zero = jnp.zeros((8, NZ), f32)
+    first = ((zero,) * 4,) * 3
     half = loop(0, CX // 2, fluxes, first, 4)
     for k in range(1, NGX):
         source = place_y * NGX + lax.rem(place_x + NGX - k, NGX)
@@ -266,10 +238,52 @@
         copy.start()
         sends.append(copy)
     loop(CX // 2, CX, fluxes, half, 4)
-    for src, dst in ((net, net_o), (cx, cx_o), (cy, cy_o), (cz, cz_o)):
+    give(cz, cz_o)
+    for copy in faces:
+        copy.wait_recv()
+
+    def face_flux(f, low, high):
+        e = f * (0.5 * ((low[0] + low[1] + low[2]) + (high[0] + high[1] + high[2])))
+        return [f * (0.5 * (low[k] + high[k])) * (low[3] - high[3]) for k in range(3)], e
+
+    live_at = lambda ids, flag: ids.astype(f32) * jnp.where(flag, 0.0, 1.0)
+    body = pl.ds(0, CY)
+    low = mobility_of(xlo_f[0], xlo_f[1], xlo_f[2]) + [xlo_f[0]]
+    high = [lam[k, 0, body, :] for k in range(3)] + [p[0, body, :]]
+    flux, e = face_flux(xlo_f[3] * live_at(xlo_i[0], place_x == 0) * live[0, body, :], low, high)
+    for k in range(3):
+        net[k, 0] = net[k, 0] - flux[k]
+    cx[0] = e
+    e4[0] = e
+    low = [lam[k, CX - 1, body, :] for k in range(3)] + [p[CX - 1, body, :]]
+    high = mobility_of(xhi_f[0], xhi_f[1], xhi_f[2]) + [xhi_f[0]]
+    flux, e = face_flux(tx[CX - 1] * live[CX - 1, body, :] * live_at(xhi_i[0], place_x == NGX - 1), low, high)
+    for k in range(3):
+        net[k, CX - 1] = net[k, CX - 1] + flux[k]
+    cx[CX] = e
+    e4[1] = e
+    low = mobility_of(ylo_f[0], ylo_f[1], ylo_f[2]) + [ylo_f[0]]
+    high = [rim[0, k] for k in range(4)]
+    flux_low, e = face_flux(ylo_f[3] * live_at(ylo_i[0], place_y == 0) * rim[0, 4], low, high)
+    e4[2] = e
+    low = [rim[1, k] for k in range(4)]
+    high = mobility_of(yhi_f[0], yhi_f[1], yhi_f[2]) + [yhi_f[0]]
+    for x in range(CX):
+        rim[0, 0, pl.ds(x, 1), :] = ty[x, pl.ds(CY - 1, 1), :]
+    flux_high, e = face_flux(rim[0, 0] * rim[1, 4] * live_at(yhi_i[0], place_y == NGY - 1), low, high)
+    e4[3] = e
+    for x in range(CX):
+        one = slice(x, x + 1)
+        first_row, last_row = pl.ds(0, 1), pl.ds(CY - 1, 1)
+        for k in range(3):
+            net[k, x, first_row, :] = net[k, x, first_row, :] - flux_low[k][one]
+            net[k, x, last_row, :] = net[k, x, last_row, :] + flux_high[k][one]
+        cy[x, first_row, :] = e4[2, pl.ds(x, 1), :]
+        cy[x, pl.ds(CY, 1), :] = e[one]
+        own4[2, pl.ds(x, 1), :] = agg[x, first_row, :]
+        own4[3, pl.ds(x, 1), :] = agg[x, last_row, :]
+    for src, dst in ((net, net_o), (cx, cx_o), (cy, cy_o)):
         give(src, dst)
-
-    zero = jnp.zeros((8, NZ), f32)
 
     def crossings(x, sums):
         sums = list(sums)
@@ -299,8 +313,6 @@
         acc[h * GROUPS + g, :] = v
         acc[g * GROUPS + h, :] = v
 
-    e4[0] = cx[0]
-    e4[1] = cx[CX]
     own4[0] = agg[0, pl.ds(0, CY), :]
     own4[1] = agg[CX - 1, pl.ds(0, CY), :]
     nb4[0] = xlo_i[1]
@@ -353,7 +365,7 @@
             face(4, f32), face(2, i32), face(3, f32), face(2, i32), face(4, f32), face(2, i32), face(3, f32), face(2, i32),
             v((3, CX + 1, CY + 8, NZ), f32), v((CX + 1, CY + 8, NZ), f32), v(BLK, f32), v((3,) + BLK, f32),
             v((3, CX, CY + 8, NZ), f32), v((CX + 1, CY, NZ), f32), v((CX, CY + 8, NZ), f32), v(BLK, f32),
-            face(10, f32), v((ROWS, NZ), f32), face(4, f32), face(4, i32), face(4, i32),
+            v((2, 5, 32, NZ), f32), v((ROWS, NZ), f32), face(4, f32), face(4, i32), face(4, i32),
             dma((8,)), dma((8,)), dma((22,)), dma((22,)), dma((NGX,)), dma((NGX,)), dma((NGY,)), dma((NGY,)),
         ],
         compiler_params=pltpu.CompilerParams(collective_id=0, has_side_effects=True, vmem_limit_bytes=BIG),
@@ -365,7 +377,7 @@
     p_h, ws_h, gs_h, old_h, pv_h, act_h, agg_h, mob_h, net_h, cx_h, cy_h, cz_h, nb_h, wells, sums,
     res_o, t_o, dinv_o, sums_o, faces_o, parts_o,
     p, ws, gs, act, agg, old, pv, net, cx, cy, cz, nb4,
-    mob, w0, w1, trows, loc, loc_s, s, rem, leak, dinv, res, t, acc, s4,
+    mob, w0, w1, trows, loc, cols, loc_s, s, rem, leak, dinv, res, t, acc, s4,
     sem, out_sem, one_sem,
 ):
     place_x, place_y = lax.axis_index("gx"), lax.axis_index("gy")
@@ -398,6 +410,7 @@
     pick = ((at_in // 32 == at_out // 32) & (at_out % 32 == 16)) | (at_out == 17)
     counts = jnp.dot(flag, jnp.where(pick, 1.0, 0.0).astype(jnp.bfloat16), preferred_element_type=f32).astype(i32)
     first_layer = pltpu.roll(layer, 18, 1)
+    cols[...] = jnp.where(here, local >> 7, -1)
     loc[...] = jnp.where(slot < PERF, local, jnp.where(slot == 18, first_layer, counts))
     to_scalar = pltpu.make_async_copy(loc, loc_s, one_sem)
     to_scalar.start()
@@ -418,23 +431,28 @@
 
                 @pl.when(loc_s[r, 32 * j + 16] > 0)
                 def _():
-                    shift = loc_s[r, 32 * j + 18] - (32 * j + PERF) + 2 * NZ
-                    shift = lax.rem(shift, NZ)
+                    top = loc_s[r, 32 * j + 18]
+                    shift = lax.rem(top - (32 * j + PERF) + 2 * NZ, NZ)
                     index_z = pltpu.roll(wells[0, pl.ds(r, 1), :], shift, 1)
                     hole_z = pltpu.roll(wells[1, pl.ds(r, 1), :], shift, 1)
+                    column_z = pltpu.roll(cols[pl.ds(r, 1), :], lax.rem(top - 32 * j + NZ, NZ), 1)
+                    column_z = jnp.where((row_lane >= top) & (row_lane < top + PERF), column_z, -1)
                     drive_z = index_z * hole_z
                     mob_z = jnp.zeros((1, NZ), f32)
                     press_z = jnp.zeros((1, NZ), f32)
+                    stores = []
                     for k in range(PERF):
-                        at = loc_s[r, 32 * j + k]
-                        z = (at & 127) | (at >> 31)
-                        q = jnp.maximum(at, 0) >> 7
-                        qx, qy = q >> 5, q & 31
-                        hit = row_lane == z
-                        w0[qx, pl.ds(qy, 1), :] += jnp.where(hit, index_z, 0.0)
-                        w1[qx, pl.ds(qy, 1), :] += jnp.where(hit, drive_z, 0.0)
-                        mob_z = jnp.where(hit, mob[qx, pl.ds(qy, 1), :], mob_z)
-                        press_z = jnp.where(hit, p[qx, pl.ds(qy, 1), :], press_z)
+                        q = jnp.maximum(loc_s[r, 32 * j + k], 0) >> 7
+                        qx, qy = q >> 5, pl.ds(q & 31, 1)
+                        hit = column_z == q
+                        stores.append((
+                            qx, qy, w0[qx, qy, :] + jnp.where(hit, index_z, 0.0), w1[qx, qy, :] + jnp.where(hit, drive_z, 0.0)
+                        ))
+                        mob_z = jnp.where(hit, mob[qx, qy, :], mob_z)
+                        press_z = jnp.where(hit, p[qx, qy, :], press_z)
+                    for qx, qy, sum0, sum1 in stores:
+                        w0[qx, qy, :] = sum0
+                        w1[qx, qy, :] = sum1
                     well = ((r & (NGX - 1)) * NGY + (r >> 3)) * 4 + j
                     trows[pl.ds(well, 1), :] = index_z * mob_z * (hole_z - press_z)
 
@@ -568,7 +586,7 @@
         scratch_shapes=[
             v(BLK, f32), v(BLK, f32), v(BLK, f32), v(BLK, i32), v(BLK, i32), v((3,) + BLK, f32), v(BLK, f32),
             v((3,) + BLK, f32), v((CX + 1, CY, NZ), f32), v((CX, CY + 8, NZ), f32), v(BLK, f32), v((4, 32, NZ), i32),
-            v(BLK, f32), v(BLK, f32), v(BLK, f32), v((4 * NDEV, NZ), f32), v((NDEV, NZ), i32), pltpu.SMEM((NDEV, NZ), i32),
+            v(BLK, f32), v(BLK, f32), v(BLK, f32), v((4 * NDEV, NZ), f32), v((NDEV, NZ), i32), v((NDEV, NZ), i32), pltpu.SMEM((NDEV, NZ), i32),
             v((CX + 2, CY + 8, NZ), f32), v(BLK, f32), v(BLK, f32), v(BLK, f32), v((3,) + BLK, f32), v(BLK, f32),
             v((NZ, NZ), f32), v((4, 32, NZ), f32),
             dma((16,)), dma((8,)), dma,
@@ -673,25 +691,34 @@
     def dot(a, b):
         return jnp.sum(jnp.sum(a * b, axis=0, keepdims=True), axis=1, keepdims=True)
 
+    def tree(values):
+        while len(values) > 1:
+            values = [a + b for a, b in zip(values[::2], values[1::2])] + values[len(values) // 2 * 2 :]
+        return values[0]
+
+    def image(v):
+        spread = [jnp.broadcast_to(v[h : h + 1, :], (8, NZ)) for h in range(GROUPS)]
+        sides = [tree([slots[pl.ds((d * GROUPS + h) * 8, 8), :] * spread[h] for h in range(GROUPS)]) for d in range(5)]
+        return tree([pltpu.roll(sides[d], moves[d], 1) for d in range(1, 5)]) + sides[0]
+
+    w = image(rhs)
+    norm = dot(rhs, rhs)
+    alpha = norm / dot(w, rhs)
+
     def one_step(_, carry):
-        x, r, q, rr = carry
-        sums5 = [None] * 5
-        for h in range(GROUPS):
-            spread = jnp.broadcast_to(q[h : h + 1, :], (8, NZ))
-            for d in range(5):
-                v = slots[pl.ds((d * GROUPS + h) * 8, 8), :] * spread
-                sums5[d] = v if sums5[d] is None else sums5[d] + v
-        image = sums5[0]
-        for d in range(1, 5):
-            image = image + pltpu.roll(sums5[d], moves[d], 1)
-        alpha = rr / dot(q, image)
+        x, r, q, aq, norm, alpha = carry
         x = x + alpha * q
-        r = r - alpha * image
+        r = r - alpha * aq
         new = dot(r, r)
-        q = r + (new / rr) * q
-        return x, r, q, new
-
-    coarse = loop(0, CITERS, one_step, (jnp.zeros((8, NZ), f32), rhs, rhs, dot(rhs, rhs)), 4)[0]
+        w = image(r)
+        curve = dot(w, r)
+        beta = new / norm
+        alpha = new / (curve - beta * (new / alpha))
+        return x, r, r + beta * q, w + beta * aq, new, alpha
+
+    start = (jnp.zeros((8, NZ), f32), rhs, rhs, w, norm, alpha)
+    x, _, q, _, _, alpha = loop(0, CITERS - 1, one_step, start, 1)
+    coarse = x + alpha * q
     mine = iota((8, NZ), 1) == me
     values = []
     for d in range(5):
@@ -769,6 +796,36 @@
     )(sums, parts, faces, t, dinv, cx, cy, cz, agg, nb4)
 
 
+def last_kernel(update_h, well, target, update_o, well_o, held, sem_in, sem_out):
+    part = CX // 4
+    moves = []
+    for n in range(4):
+        at = pl.ds(part * n, part)
+        copy = pltpu.make_async_copy(update_h.at[at], held.at[at], sem_in.at[n])
+        copy.start()
+        moves.append((copy, pltpu.make_async_copy(held.at[at], update_o.at[at], sem_out.at[n])))
+    for j in range(4):
+        well_o[j] = well[0, j] - target[j]
+    for arrive, leave in moves:
+        arrive.wait()
+        leave.start()
+    for _, leave in moves:
+        leave.wait()
+
+
+def last_part(update, well, target):
+    sds = jax.ShapeDtypeStruct
+    return pl.pallas_call(
+        last_kernel,
+        out_shape=[sds(BLK, f32), sds((4,), f32)],
+        in_specs=[ANY, SMEM, SMEM],
+        out_specs=[ANY, SMEM],
+        scratch_shapes=[pltpu.VMEM(BLK, f32), pltpu.SemaphoreType.DMA((4,)), pltpu.SemaphoreType.DMA((4,))],
+        compiler_params=pltpu.CompilerParams(vmem_limit_bytes=BIG),
+        name="last",
+    )(update, well, target)
+
+
 def per_device(
     pressure, water_sat, gas_sat, old_content, pore_volume, trans_x, trans_y, trans_z, active, aggregate,
     well_cells, well_index, bottom_hole, well_target,
@@ -780,7 +837,8 @@
         pressure, water_sat, gas_sat, old_content, pore_volume, active, aggregate, mob, net, cx, cy, cz, nb, wells, sums
     )
     update, well = coarse_part(sums, parts, faces, t, dinv, cx, cy, cz, aggregate, nb)
-    return residual, update, well[0, :4] - well_target
+    update, well_residual = last_part(update, well, well_target)
+    return residual, update, well_residual
 
 
 def solution(mesh):

time: 59.8 us -> 54.2 us (0.906)
  Pallas kernels: 55.9 us -> 53.3 us
  local copies, waits for them, and re-layouts: 1.87 us -> 0 us
  other arithmetic: 1.09 us -> 0 us
    pallas_call x1, Pallas kernels: 22.7 us -> 18.7 us  [coarse_part(): pl.pallas_call(coarse_kernel, out_shape=[sds(BLK, f32), sds((1, NZ), f32)...]
    pallas_call x0 -> x1, Pallas kernels: none -> 3.01 us  [last_part(): pl.pallas_call(last_kernel, out_shape=[sds(BLK, f32), sds((4,), f32)], in...]
    pallas_call x1, Pallas kernels: 23.6 us -> 21.3 us  [exchange(): pl.pallas_call(exchange_kernel, out_shape=[sds((3,) + BLK, f32), sds((CX...]
    unnamed x3 -> x0, local copies, waits for them, and re-layouts: 1.87 us -> none
    sub x1 -> x0, other arithmetic: 1.09 us -> none  [per_device(): return (residual, update, well[0, :4] - well_target)]
    pallas_call x1, Pallas kernels: 9.67 us -> 10.3 us  [local(): pl.pallas_call(local_kernel, out_shape=[sds((3,) + BLK, f32), sds(BLK, f3...]
where the time goes in v3:
time: 54.2 us; the launch traced here: 54 us
  Pallas kernels  53.3 us (98%)
  between operations  0.66 us (1%)
    pallas_call x1, Pallas kernels, exchange(): pl.pallas_call(exchange_kernel, out_shape=[sds((3,) + BLK, f32), sds((CX...  21.3 us
    pallas_call x1, Pallas kernels, coarse_part(): pl.pallas_call(coarse_kernel, out_shape=[sds(BLK, f32), sds((1, NZ), f32)...  18.7 us
    pallas_call x1, Pallas kernels, local(): pl.pallas_call(local_kernel, out_shape=[sds((3,) + BLK, f32), sds(BLK, f3...  10.3 us
    pallas_call x1, Pallas kernels, last_part(): pl.pallas_call(last_kernel, out_shape=[sds(BLK, f32), sds((4,), f32)], in...  3.01 us

profile of v3, /device:TPU:1, one launch (start us, length us, event | category | flops | bytes accessed | tf_op | source)
XLA Modules:
  0.0 54.0 jit_solution(583803819358285492)
XLA Ops:
  0.6 21.3 %exchange.1 = (f32[3,32,32,128]{3,2,1,0:T(8,128)}, f32[33,32,128]{2,1,0:T(8,128)}, f32[32,40,128]{2,1,0:T(8,128)}, f32[32,32,128]{2,1,0:T(8,128)}, f32[32,32,128...) custom-call(f32[32,32,128]{2,1,0:T(8,128)} %p_h.3, f32[32,32,128]{2,1,0:T(8,128)} %ws_h.3, ...), custom_call_target="tpu_custom_call" | custom-call | tf_op jit(solution)/shard_map/exchange/pallas_call | solution.py:354
  21.9 10.3 %local.1 = (f32[3,32,32,128]{3,2,1,0:T(8,128)}, f32[32,32,128]{2,1,0:T(8,128)}, f32[32,32,128]{2,1,0:T(8,128)}, f32[3,1,128]{2,1,0:T(1,128)}, f32[4,32,128]{2,1,0:T(8,128)}, /*index=5*/f32[8,128]{1,0:T(8,128)}) custom-call(f32[32,32,128]{2,1,0:T(8,128)} %p_h.3, f32[32,32,128]{2,1,0:T(8,128)} %ws_h.3, f32[32,32,128]{2,1,0:T(8,128)} %gs_h.3, ...), custom_call_target="tpu_custom_call" | custom-call | tf_op jit(solution)/shard_map/local/pallas_call | solution.py:579
  32.2 18.7 %coarse.1 = (f32[32,32,128]{2,1,0:T(8,128)}, f32[1,128]{1,0:T(1,128)}) custom-call(f32[3,1,128]{2,1,0:T(1,128)} %get-tuple-element.30.sums, f32[8,128]{1,0:T(8,128)} %get-tuple-element.31.parts, f32[4,32,128]{2,1,0:T(8,128)} %get-tuple-element.32.faces, f32[32,32,128]{2,1,0:T(8,128)} %get-tuple-element.33.t_h, f32[32,32,128]{2,1,0:T(8,128)} %get-tuple-element.34.dinv_h, ...), custom_call_target="tpu_custom_call" | custom-call | tf_op jit(solution)/shard_map/coarse/pallas_call | solution.py:780
  51.0 3.0 %last.1 = (f32[32,32,128]{2,1,0:T(8,128)}, f32[4]{0:T(128)}) custom-call(f32[32,32,128]{2,1,0:T(8,128)} %get-tuple-element.35.update_h, f32[1,128]{1,0:T(1,128)} %get-tuple-element.36.well, f32[4]{0:T(128)} %target.1), custom_call_target="tpu_custom_call" | custom-call | tf_op jit(solution)/shard_map/last/pallas_call | solution.py:818

commit v4 on v3

--- a/solution.py
+++ b/solution.py
@@ -82,10 +82,10 @@
 
 
 def exchange_kernel(
-    p_h, ws_h, gs_h, act_h, tx_h, ty_h, tz_h, agg_h, cells, windex, hole,
+    p_h, ws_h, gs_h, act_h, tx_h, ty_h, tz_h, agg_h, cells_h, windex_h, hole_h,
     net_o, cx_o, cy_o, cz_o, mob_o, sums_o, nb_o, wells,
     p, ws, gs, act, tx, ty, tz, agg, xlo_f, xlo_i, xhi_f, xhi_i, ylo_f, ylo_i, yhi_f, yhi_i,
-    lam, live, mob, net, fy, cx, cy, cz, rim, acc, e4, own4, nb4,
+    lam, live, mob, net, fy, cx, cy, cz, rim, acc, e4, own4, nb4, cells, windex, hole,
     load_sem, out_sem, face_send, face_recv, send_x, recv_x, send_y, recv_y,
 ):
     place_x, place_y = lax.axis_index("gx"), lax.axis_index("gy")
@@ -94,11 +94,14 @@
     greet(barrier)
     loads = []
     for src, dst in (
+        (cells_h, cells), (windex_h, windex), (hole_h, hole),
         (p_h, p.at[BODY]), (ws_h, ws), (gs_h, gs), (act_h, act), (tx_h, tx), (ty_h, ty), (tz_h, tz), (agg_h, agg.at[BODY])
     ):
         copy = pltpu.make_async_copy(src, dst, load_sem.at[len(loads)])
         copy.start()
         loads.append(copy)
+    for copy in loads[:3]:
+        copy.wait()
     lane = iota((1, NZ), 1)
     pad = lambda v: jnp.concatenate([v, jnp.zeros((4, NZ - PERF), f32)], axis=1)
     both = pad(cells[...].astype(f32)) + pltpu.roll(pad(windex[...]), PERF, 1)
@@ -144,7 +147,7 @@
     for copy in sends + faces:
         copy.start()
 
-    for copy in loads[:4]:
+    for copy in loads[3:7]:
         copy.wait()
 
     def mobilities(x, _):
@@ -184,7 +187,7 @@
         outs.append(copy)
 
     give(mob, mob_o)
-    for copy in loads[4:]:
+    for copy in loads[7:]:
         copy.wait()
     layer_8 = iota((8, NZ), 1)
     row_8 = iota((8, NZ), 0)
@@ -357,7 +360,7 @@
             sds((3,) + BLK, f32), sds((CX + 1, CY, NZ), f32), sds((CX, CY + 8, NZ), f32), sds(BLK, f32), sds(BLK, f32),
             sds((3, 1, NZ), f32), sds((4, 32, NZ), i32), sds((2, NDEV, NZ), f32),
         ],
-        in_specs=[ANY] * 8 + [VMEM, VMEM, SMEM],
+        in_specs=[ANY] * 11,
         out_specs=[ANY] * 5 + [VMEM, ANY, VMEM],
         scratch_shapes=[
             v((CX + 1, CY + 8, NZ), f32), v(BLK, f32), v(BLK, f32), v(BLK, i32),
@@ -366,7 +369,8 @@
             v((3, CX + 1, CY + 8, NZ), f32), v((CX + 1, CY + 8, NZ), f32), v(BLK, f32), v((3,) + BLK, f32),
             v((3, CX, CY + 8, NZ), f32), v((CX + 1, CY, NZ), f32), v((CX, CY + 8, NZ), f32), v(BLK, f32),
             v((2, 5, 32, NZ), f32), v((ROWS, NZ), f32), face(4, f32), face(4, i32), face(4, i32),
-            dma((8,)), dma((8,)), dma((22,)), dma((22,)), dma((NGX,)), dma((NGX,)), dma((NGY,)), dma((NGY,)),
+            v((4, PERF), i32), v((4, PERF), f32), pltpu.SMEM((4,), f32),
+            dma((11,)), dma((8,)), dma((22,)), dma((22,)), dma((NGX,)), dma((NGX,)), dma((NGY,)), dma((NGY,)),
         ],
         compiler_params=pltpu.CompilerParams(collective_id=0, has_side_effects=True, vmem_limit_bytes=BIG),
         name="exchange",
@@ -374,10 +378,10 @@
 
 
 def local_kernel(
-    p_h, ws_h, gs_h, old_h, pv_h, act_h, agg_h, mob_h, net_h, cx_h, cy_h, cz_h, nb_h, wells, sums,
+    p_h, ws_h, gs_h, old_h, pv_h, act_h, agg_h, mob_h, net_h, cx_h, cy_h, cz_h, nb_h, wells_h, sums_h,
     res_o, t_o, dinv_o, sums_o, faces_o, parts_o,
     p, ws, gs, act, agg, old, pv, net, cx, cy, cz, nb4,
-    mob, w0, w1, trows, loc, cols, loc_s, s, rem, leak, dinv, res, t, acc, s4,
+    mob, w0, w1, trows, loc, cols, loc_s, s, rem, leak, dinv, res, t, acc, s4, wells, sums, parts_v,
     sem, out_sem, one_sem,
 ):
     place_x, place_y = lax.axis_index("gx"), lax.axis_index("gy")
@@ -388,15 +392,17 @@
         copy.start()
         copies.append(copy)
 
+    fetch(wells_h, wells)
     fetch(mob_h, mob)
     fetch(p_h, p)
     early = len(copies)
     for src, dst in (
         (ws_h, ws), (gs_h, gs), (act_h, act), (pv_h, pv), (old_h, old), (net_h, net), (cx_h, cx), (cy_h, cy), (cz_h, cz),
-        (agg_h, agg), (nb_h, nb4),
+        (agg_h, agg), (nb_h, nb4), (sums_h, sums),
     ):
         fetch(src, dst)
 
+    copies[0].wait()
     lane = iota((NDEV, NZ), 1)
     table = wells[0]
     cell = table.astype(i32)
@@ -418,7 +424,7 @@
     w0[...] = jnp.zeros_like(w0)
     w1[...] = jnp.zeros_like(w1)
     trows[...] = jnp.zeros_like(trows)
-    for copy in copies[:early]:
+    for copy in copies[1:early]:
         copy.wait()
     to_scalar.wait()
 
@@ -469,7 +475,7 @@
         if k % 2:
             piece = pltpu.roll(piece, 64, 1)
         parts = jnp.where(sub == k, piece, parts)
-    parts_o[...] = parts
+    parts_v[...] = parts
 
     for copy in copies[early:]:
         copy.wait()
@@ -523,6 +529,7 @@
     give(res, res_o)
     give(dinv, dinv_o)
     give(s4, faces_o)
+    give(parts_v, parts_o)
 
     zero = jnp.zeros((8, NZ), f32)
 
@@ -565,9 +572,8 @@
     first = RHS_AT - 2 * NZ
     for n in range(6):
         acc[pl.ds(first + 8 * n, 8), :] = jnp.concatenate(rows[8 * n : 8 * n + 8], axis=0)
-    sums_o[0] = sums[0]
-    sums_o[1] = sums[1]
-    sums_o[2] = sums[2] + jnp.sum(acc[...].T, axis=0, keepdims=True)
+    sums[2] = sums[2] + jnp.sum(acc[...].T, axis=0, keepdims=True)
+    give(sums, sums_o)
     for copy in outs:
         copy.wait()
 
@@ -581,14 +587,14 @@
         out_shape=[
             sds((3,) + BLK, f32), sds(BLK, f32), sds(BLK, f32), sds((3, 1, NZ), f32), sds((4, 32, NZ), f32), sds((8, NZ), f32)
         ],
-        in_specs=[ANY] * 13 + [VMEM, VMEM],
-        out_specs=[ANY] * 3 + [VMEM, ANY, VMEM],
+        in_specs=[ANY] * 15,
+        out_specs=[ANY] * 6,
         scratch_shapes=[
             v(BLK, f32), v(BLK, f32), v(BLK, f32), v(BLK, i32), v(BLK, i32), v((3,) + BLK, f32), v(BLK, f32),
             v((3,) + BLK, f32), v((CX + 1, CY, NZ), f32), v((CX, CY + 8, NZ), f32), v(BLK, f32), v((4, 32, NZ), i32),
             v(BLK, f32), v(BLK, f32), v(BLK, f32), v((4 * NDEV, NZ), f32), v((NDEV, NZ), i32), v((NDEV, NZ), i32), pltpu.SMEM((NDEV, NZ), i32),
             v((CX + 2, CY + 8, NZ), f32), v(BLK, f32), v(BLK, f32), v(BLK, f32), v((3,) + BLK, f32), v(BLK, f32),
-            v((NZ, NZ), f32), v((4, 32, NZ), f32),
+            v((NZ, NZ), f32), v((4, 32, NZ), f32), v((2, NDEV, NZ), f32), v((3, 1, NZ), f32), v((8, NZ), f32),
             dma((16,)), dma((8,)), dma,
         ],
         compiler_params=pltpu.CompilerParams(vmem_limit_bytes=BIG),
@@ -597,9 +603,9 @@
 
 
 def coarse_kernel(
-    sums, parts, faces, t_h, dinv_h, cx_h, cy_h, cz_h, agg_h, nb4,
+    sums_h, parts_h, faces, t_h, dinv_h, cx_h, cy_h, cz_h, agg_h, nb_h, target,
     update_o, well_o,
-    gather, mat, slots, send_rows, rows_x, rows_y, tall, dinv, cx, cy, cz, agg, far, pc,
+    gather, mat, slots, send_rows, rows_x, rows_y, tall, dinv, cx, cy, cz, agg, far, pc, sums, parts, nb4,
     sem, send_x, recv_x, send_y, recv_y, psend_x, precv_x, psend_y, precv_y, fsend, frecv,
 ):
     place_x, place_y = lax.axis_index("gx"), lax.axis_index("gy")
@@ -608,10 +614,12 @@
     greet(barrier)
     loads = []
     body = (slice(None), pl.ds(0, CY), slice(None))
-    for src, dst in ((t_h, tall), (dinv_h, dinv), (cx_h, cx), (cy_h, cy), (cz_h, cz), (agg_h, agg)):
+    for src, dst in ((sums_h, sums), (parts_h, parts), (nb_h, nb4), (t_h, tall), (dinv_h, dinv), (cx_h, cx), (cy_h, cy), (cz_h, cz), (agg_h, agg)):
         copy = pltpu.make_async_copy(src, dst, sem.at[len(loads)])
         copy.start()
         loads.append(copy)
+    for copy in loads[:2]:
+        copy.wait()
     for n in range(3):
         gather[n, pl.ds(me, 1), :] = sums[n]
     rows_x[pl.ds(place_x, 1), :] = parts[pl.ds(place_x, 1), :]
@@ -733,7 +741,7 @@
 
     for copy in halo:
         copy.wait_recv()
-    for copy in loads:
+    for copy in loads[2:]:
         copy.wait()
     pc[0, pl.ds(8, CY), :] = far[0] + look_up(nb4[0], 1)
     pc[CX + 1, pl.ds(8, CY), :] = far[1] + look_up(nb4[1], 2)
@@ -768,62 +776,66 @@
         source = lax.rem(place_y + NGY - k, NGY)
         there = rows_y.at[pl.ds(source, 1), :]
         remote(there, there, psend_y.at[k], precv_y.at[k], place_x, place_y).wait_recv()
-    well_o[...] = jnp.sum(rows_y[...], axis=0, keepdims=True)
+    rates = jnp.sum(rows_y[...], axis=0, keepdims=True)
+    for j in range(4):
+        well_o[j] = rates[0, j] - target[j]
     for copy in sends + halo:
         copy.wait_send()
 
 
-def coarse_part(sums, parts, faces, t, dinv, cx, cy, cz, agg, nb4):
+def coarse_part(sums, parts, faces, t, dinv, cx, cy, cz, agg, nb4, target):
     v = pltpu.VMEM
     sds = jax.ShapeDtypeStruct
     dma = pltpu.SemaphoreType.DMA
     return pl.pallas_call(
         coarse_kernel,
-        out_shape=[sds(BLK, f32), sds((1, NZ), f32)],
-        in_specs=[VMEM, VMEM, ANY] + [ANY] * 6 + [VMEM],
-        out_specs=[VMEM, VMEM],
+        out_shape=[sds(BLK, f32), sds((4,), f32)],
+        in_specs=[ANY] * 10 + [SMEM],
+        out_specs=[VMEM, SMEM],
         scratch_shapes=[
             v((3, NDEV, NZ), f32), v((ROWS, NZ), f32), v((5 * 64, NZ), f32), v((NGY, NZ), f32), v((NGX, NZ), f32), v((NGY, NZ), f32),
             v(BLK, f32), v(BLK, f32), v((CX + 1, CY, NZ), f32), v((CX, CY + 8, NZ), f32), v(BLK, f32), v(BLK, i32),
             v((4, 32, NZ), f32), v((CX + 2, CY + 16, NZ), f32),
-            dma((8,)), dma((NGX,)), dma((NGX,)), dma((NGY,)), dma((NGY,)),
+            v((3, 1, NZ), f32), v((8, NZ), f32), v((4, 32, NZ), i32),
+            dma((9,)), dma((NGX,)), dma((NGX,)), dma((NGY,)), dma((NGY,)),
             dma((NGX,)), dma((NGX,)), dma((NGY,)), dma((NGY,)), dma((4,)), dma((4,)),
         ],
         compiler_params=pltpu.CompilerParams(
             collective_id=1, has_side_effects=True, vmem_limit_bytes=BIG
         ),
         name="coarse",
-    )(sums, parts, faces, t, dinv, cx, cy, cz, agg, nb4)
-
-
-def last_kernel(update_h, well, target, update_o, well_o, held, sem_in, sem_out):
+    )(sums, parts, faces, t, dinv, cx, cy, cz, agg, nb4, target)
+
+
+def last_kernel(update_h, well_h, update_o, well_o, held, sem_in, sem_out, well_sem):
     part = CX // 4
     moves = []
+    well = pltpu.make_async_copy(well_h, well_o, well_sem)
+    well.start()
     for n in range(4):
         at = pl.ds(part * n, part)
         copy = pltpu.make_async_copy(update_h.at[at], held.at[at], sem_in.at[n])
         copy.start()
         moves.append((copy, pltpu.make_async_copy(held.at[at], update_o.at[at], sem_out.at[n])))
-    for j in range(4):
-        well_o[j] = well[0, j] - target[j]
     for arrive, leave in moves:
         arrive.wait()
         leave.start()
     for _, leave in moves:
         leave.wait()
-
-
-def last_part(update, well, target):
+    well.wait()
+
+
+def last_part(update, well):
     sds = jax.ShapeDtypeStruct
     return pl.pallas_call(
         last_kernel,
         out_shape=[sds(BLK, f32), sds((4,), f32)],
-        in_specs=[ANY, SMEM, SMEM],
-        out_specs=[ANY, SMEM],
-        scratch_shapes=[pltpu.VMEM(BLK, f32), pltpu.SemaphoreType.DMA((4,)), pltpu.SemaphoreType.DMA((4,))],
+        in_specs=[ANY, ANY],
+        out_specs=[ANY, ANY],
+        scratch_shapes=[pltpu.VMEM(BLK, f32), pltpu.SemaphoreType.DMA((4,)), pltpu.SemaphoreType.DMA((4,)), pltpu.SemaphoreType.DMA],
         compiler_params=pltpu.CompilerParams(vmem_limit_bytes=BIG),
         name="last",
-    )(update, well, target)
+    )(update, well)
 
 
 def per_device(
@@ -836,8 +848,8 @@
     residual, t, dinv, sums, faces, parts = local(
         pressure, water_sat, gas_sat, old_content, pore_volume, active, aggregate, mob, net, cx, cy, cz, nb, wells, sums
     )
-    update, well = coarse_part(sums, parts, faces, t, dinv, cx, cy, cz, aggregate, nb)
-    update, well_residual = last_part(update, well, well_target)
+    update, well = coarse_part(sums, parts, faces, t, dinv, cx, cy, cz, aggregate, nb, well_target)
+    update, well_residual = last_part(update, well)
     return residual, update, well_residual
 
 

time: 54.2 us -> 51.5 us (0.950)
  Pallas kernels: 53.3 us -> 50.3 us
    pallas_call x1, Pallas kernels: 10.3 us -> 8.8 us  [local(): pl.pallas_call(local_kernel, out_shape=[sds((3,) + BLK, f32), sds(BLK, f3...]
    pallas_call x1, Pallas kernels: 3.01 us -> 1.83 us  [last_part(): pl.pallas_call(last_kernel, out_shape=[sds(BLK, f32), sds((4,), f32)], in...]
    pallas_call x1, Pallas kernels: 21.3 us -> 20.5 us  [exchange(): pl.pallas_call(exchange_kernel, out_shape=[sds((3,) + BLK, f32), sds((CX...]
where the time goes in v4:
time: 51.5 us; the launch traced here: 51 us
  Pallas kernels  50.3 us (98%)
  between operations  0.66 us (1%)
    pallas_call x1, Pallas kernels, exchange(): pl.pallas_call(exchange_kernel, out_shape=[sds((3,) + BLK, f32), sds((CX...  20.5 us
    pallas_call x1, Pallas kernels, coarse_part(): pl.pallas_call(coarse_kernel, out_shape=[sds(BLK, f32), sds((4,), f32)],...  19.2 us
    pallas_call x1, Pallas kernels, local(): pl.pallas_call(local_kernel, out_shape=[sds((3,) + BLK, f32), sds(BLK, f3...  8.8 us
    pallas_call x1, Pallas kernels, last_part(): pl.pallas_call(last_kernel, out_shape=[sds(BLK, f32), sds((4,), f32)], in...  1.83 us

profile of v4, /device:TPU:1, one launch (start us, length us, event | category | flops | bytes accessed | tf_op | source)
XLA Modules:
  0.0 51.0 jit_solution(16086479283585261141)
XLA Ops:
  0.6 20.5 %exchange.1 = (f32[3,32,32,128]{3,2,1,0:T(8,128)}, f32[33,32,128]{2,1,0:T(8,128)}, f32[32,40,128]{2,1,0:T(8,128)}, f32[32,32,128]{2,1,0:T(8,128)}, f32[32,32,128...) custom-call(f32[32,32,128]{2,1,0:T(8,128)} %p_h.3, f32[32,32,128]{2,1,0:T(8,128)} %ws_h.3, ...), custom_call_target="tpu_custom_call" | custom-call | tf_op jit(solution)/shard_map/exchange/pallas_call | solution.py:357
  21.1 8.8 %local.1 = (f32[3,32,32,128]{3,2,1,0:T(8,128)}, f32[32,32,128]{2,1,0:T(8,128)}, f32[32,32,128]{2,1,0:T(8,128)}, f32[3,1,128]{2,1,0:T(1,128)}, f32[4,32,128]{2,1,0:T(8,128)}, /*index=5*/f32[8,128]{1,0:T(8,128)}) custom-call(f32[32,32,128]{2,1,0:T(8,128)} %p_h.3, f32[32,32,128]{2,1,0:T(8,128)} %ws_h.3, f32[32,32,128]{2,1,0:T(8,128)} %gs_h.3, ...), custom_call_target="tpu_custom_call" | custom-call | tf_op jit(solution)/shard_map/local/pallas_call | solution.py:585
  30.0 19.2 %coarse.1 = (f32[32,32,128]{2,1,0:T(8,128)}, f32[4]{0:T(128)}) custom-call(f32[3,1,128]{2,1,0:T(1,128)} %get-tuple-element.30.sums_h, f32[8,128]{1,0:T(8,128)} %get-tuple-element.31.parts_h, f32[4,32,128]{2,1,0:T(8,128)} %get-tuple-element.32.faces, f32[32,32,128]{2,1,0:T(8,128)} %get-tuple-element.33.t_h, f32[32,32,128]{2,1,0:T(8,128)} %get-tuple-element.34.dinv_h, ...), custom_call_target="tpu_custom_call" | custom-call | tf_op jit(solution)/shard_map/coarse/pallas_call | solution.py:790
  49.1 1.8 %last.1 = (f32[32,32,128]{2,1,0:T(8,128)}, f32[4]{0:T(128)}) custom-call(f32[32,32,128]{2,1,0:T(8,128)} %get-tuple-element.35.update_h, f32[4]{0:T(128)} %get-tuple-element.36.well_h), custom_call_target="tpu_custom_call" | custom-call | tf_op jit(solution)/shard_map/last/pallas_call | solution.py:830

commit v5 on v4

--- a/solution.py
+++ b/solution.py
@@ -605,8 +605,8 @@
 def coarse_kernel(
     sums_h, parts_h, faces, t_h, dinv_h, cx_h, cy_h, cz_h, agg_h, nb_h, target,
     update_o, well_o,
-    gather, mat, slots, send_rows, rows_x, rows_y, tall, dinv, cx, cy, cz, agg, far, pc, sums, parts, nb4,
-    sem, send_x, recv_x, send_y, recv_y, psend_x, precv_x, psend_y, precv_y, fsend, frecv,
+    gather, mat, slots, send_rows, rows_x, rows_y, tall, dinv, cx, cy, cz, agg, far, pc, sums, parts, nb4, update,
+    sem, leave_sem, send_x, recv_x, send_y, recv_y, psend_x, precv_x, psend_y, precv_y, fsend, frecv,
 ):
     place_x, place_y = lax.axis_index("gx"), lax.axis_index("gy")
     me = place_y * NGX + place_x
@@ -768,10 +768,16 @@
                 + cy[x, at, :] * pc[x + 1, pl.ds(8 * c + 7, 8), :]
             )
             near = near + (z * lane_next(here) + lane_prev(z * here))
-            update_o[x, at, :] = tall[x, at, :] + (1.0 - relax) * here + dinv[x, at, :] * near
+            update[x, at, :] = tall[x, at, :] + (1.0 - relax) * here + dinv[x, at, :] * near
         return 0
 
-    loop(0, CX, finish, 0, 8)
+    leaves = []
+    for n in range(4):
+        loop(8 * n, 8 * n + 8, finish, 0, 8)
+        at = pl.ds(8 * n, 8)
+        copy = pltpu.make_async_copy(update.at[at], update_o.at[at], leave_sem.at[n])
+        copy.start()
+        leaves.append(copy)
     for k in range(1, NGY):
         source = lax.rem(place_y + NGY - k, NGY)
         there = rows_y.at[pl.ds(source, 1), :]
@@ -781,6 +787,8 @@
         well_o[j] = rates[0, j] - target[j]
     for copy in sends + halo:
         copy.wait_send()
+    for copy in leaves:
+        copy.wait()
 
 
 def coarse_part(sums, parts, faces, t, dinv, cx, cy, cz, agg, nb4, target):
@@ -791,13 +799,13 @@
         coarse_kernel,
         out_shape=[sds(BLK, f32), sds((4,), f32)],
         in_specs=[ANY] * 10 + [SMEM],
-        out_specs=[VMEM, SMEM],
+        out_specs=[ANY, SMEM],
         scratch_shapes=[
             v((3, NDEV, NZ), f32), v((ROWS, NZ), f32), v((5 * 64, NZ), f32), v((NGY, NZ), f32), v((NGX, NZ), f32), v((NGY, NZ), f32),
             v(BLK, f32), v(BLK, f32), v((CX + 1, CY, NZ), f32), v((CX, CY + 8, NZ), f32), v(BLK, f32), v(BLK, i32),
             v((4, 32, NZ), f32), v((CX + 2, CY + 16, NZ), f32),
-            v((3, 1, NZ), f32), v((8, NZ), f32), v((4, 32, NZ), i32),
-            dma((9,)), dma((NGX,)), dma((NGX,)), dma((NGY,)), dma((NGY,)),
+            v((3, 1, NZ), f32), v((8, NZ), f32), v((4, 32, NZ), i32), v(BLK, f32),
+            dma((9,)), dma((4,)), dma((NGX,)), dma((NGX,)), dma((NGY,)), dma((NGY,)),
             dma((NGX,)), dma((NGX,)), dma((NGY,)), dma((NGY,)), dma((4,)), dma((4,)),
         ],
         compiler_params=pltpu.CompilerParams(

time: 51.5 us -> 51.4 us (level)
    pallas_call x1, Pallas kernels: 8.8 us -> 9.46 us  [local(): pl.pallas_call(local_kernel, out_shape=[sds((3,) + BLK, f32), sds(BLK, f3...]
    pallas_call x1, Pallas kernels: 19.2 us -> 18.6 us  [coarse_part(): pl.pallas_call(coarse_kernel, out_shape=[sds(BLK, f32), sds((4,), f32)],...]
where the time goes in v5:
time: 51.4 us; the launch traced here: 51.1 us
  Pallas kernels  50.4 us (98%)
  between operations  0.66 us (1%)
    pallas_call x1, Pallas kernels, exchange(): pl.pallas_call(exchange_kernel, out_shape=[sds((3,) + BLK, f32), sds((CX...  20.5 us
    pallas_call x1, Pallas kernels, coarse_part(): pl.pallas_call(coarse_kernel, out_shape=[sds(BLK, f32), sds((4,), f32)],...  18.6 us
    pallas_call x1, Pallas kernels, local(): pl.pallas_call(local_kernel, out_shape=[sds((3,) + BLK, f32), sds(BLK, f3...  9.46 us
    pallas_call x1, Pallas kernels, last_part(): pl.pallas_call(last_kernel, out_shape=[sds(BLK, f32), sds((4,), f32)], in...  1.83 us

profile of v5, /device:TPU:1, one launch (start us, length us, event | category | flops | bytes accessed | tf_op | source)
XLA Modules:
  0.0 51.1 jit_solution(9641634483278228883)
XLA Ops:
  0.6 20.5 %exchange.1 = (f32[3,32,32,128]{3,2,1,0:T(8,128)}, f32[33,32,128]{2,1,0:T(8,128)}, f32[32,40,128]{2,1,0:T(8,128)}, f32[32,32,128]{2,1,0:T(8,128)}, f32[32,32,128...) custom-call(f32[32,32,128]{2,1,0:T(8,128)} %p_h.3, f32[32,32,128]{2,1,0:T(8,128)} %ws_h.3, ...), custom_call_target="tpu_custom_call" | custom-call | tf_op jit(solution)/shard_map/exchange/pallas_call | solution.py:357
  21.1 9.5 %local.1 = (f32[3,32,32,128]{3,2,1,0:T(8,128)}, f32[32,32,128]{2,1,0:T(8,128)}, f32[32,32,128]{2,1,0:T(8,128)}, f32[3,1,128]{2,1,0:T(1,128)}, f32[4,32,128]{2,1,0:T(8,128)}, /*index=5*/f32[8,128]{1,0:T(8,128)}) custom-call(f32[32,32,128]{2,1,0:T(8,128)} %p_h.3, f32[32,32,128]{2,1,0:T(8,128)} %ws_h.3, f32[32,32,128]{2,1,0:T(8,128)} %gs_h.3, ...), custom_call_target="tpu_custom_call" | custom-call | tf_op jit(solution)/shard_map/local/pallas_call | solution.py:585
  30.6 18.6 %coarse.1 = (f32[32,32,128]{2,1,0:T(8,128)}, f32[4]{0:T(128)}) custom-call(f32[3,1,128]{2,1,0:T(1,128)} %get-tuple-element.30.sums_h, f32[8,128]{1,0:T(8,128)} %get-tuple-element.31.parts_h, f32[4,32,128]{2,1,0:T(8,128)} %get-tuple-element.32.faces, f32[32,32,128]{2,1,0:T(8,128)} %get-tuple-element.33.t_h, f32[32,32,128]{2,1,0:T(8,128)} %get-tuple-element.34.dinv_h, ...), custom_call_target="tpu_custom_call" | custom-call | tf_op jit(solution)/shard_map/coarse/pallas_call | solution.py:798
  49.3 1.8 %last.1 = (f32[32,32,128]{2,1,0:T(8,128)}, f32[4]{0:T(128)}) custom-call(f32[32,32,128]{2,1,0:T(8,128)} %get-tuple-element.35.update_h, f32[4]{0:T(128)} %get-tuple-element.36.well_h), custom_call_target="tpu_custom_call" | custom-call | tf_op jit(solution)/shard_map/last/pallas_call | solution.py:838
